TPU v7x, 128 devices: a whole 4x4x4 slice. The times are simulated.
128 devices in a mesh: fsdp: 4 (over x), ctx: 16 (over z_hi, y, core), tp: 2 (over z_lo).
Axes of the slice: x: 4, y: 4, z: 4 (z_hi: 2, z_lo: 2; z = z_hi * 2 + z_lo), core: 2. Of those that a mesh axis runs over, the one named last changes fastest.
Arguments:
- tokens: bfloat16 [4, 4096, 1024], P('fsdp', 'ctx'), may hold values from -12 to 12, as said below
- ln1_gain: bfloat16 [1024], P(('fsdp', 'ctx')), may hold values from 0.5 to 1.5
- ln1_bias: bfloat16 [1024], P(('fsdp', 'ctx')), may hold values from -1.5 to 1.5
- qkv_weight: bfloat16 [1024, 3, 1024], P(('fsdp', 'ctx'), None, 'tp'), may hold values from -0.1875 to 0.1875
- qv_bias: bfloat16 [2, 1024], P(None, 'tp'), may hold values from -1.5 to 1.5
- proj_weight: bfloat16 [1024, 1024], P('tp', ('fsdp', 'ctx')), may hold values from -0.75 to 0.75
- proj_bias: bfloat16 [1024], P(('fsdp', 'ctx')), may hold values from -1.5 to 1.5
- ln2_gain: bfloat16 [1024], P(('fsdp', 'ctx')), may hold values from 0.5 to 1.5
- ln2_bias: bfloat16 [1024], P(('fsdp', 'ctx')), may hold values from -1.5 to 1.5
- fc_weight: bfloat16 [1024, 4096], P(('fsdp', 'ctx'), 'tp'), may hold values from -0.1875 to 0.1875
- fc_bias: bfloat16 [4096], P('tp'), may hold values from -2.5 to 2.5
- out_weight: bfloat16 [4096, 1024], P('tp', ('fsdp', 'ctx')), may hold values from -0.09375 to 0.09375
- out_bias: bfloat16 [1024], P(('fsdp', 'ctx')), may hold values from -1.5 to 1.5
- piece_starts: int32 [4, 2], P('fsdp'), may hold values from 0 to 3840, as said below
- seq_lengths: int32 [4], replicated, may hold values from 3968 to 4096, as said below
- cotangent: bfloat16 [4, 4096, 1024], P('fsdp', 'ctx'), may hold values from -6 to 6
Outputs:
- layer_out: bfloat16 [4, 4096, 1024], P('fsdp', 'ctx')
- grad_tokens: bfloat16 [4, 4096, 1024], P('fsdp', 'ctx')
- grad_ln1_gain: float32 [1024], P(('fsdp', 'ctx'))
- grad_ln1_bias: float32 [1024], P(('fsdp', 'ctx'))
- grad_qkv: float32 [1024, 3, 1024], P(('fsdp', 'ctx'), None, 'tp')
- grad_qv_bias: float32 [2, 1024], P(None, 'tp')
- grad_proj: float32 [1024, 1024], P('tp', ('fsdp', 'ctx'))
- grad_proj_bias: float32 [1024], P(('fsdp', 'ctx'))
- grad_ln2_gain: float32 [1024], P(('fsdp', 'ctx'))
- grad_ln2_bias: float32 [1024], P(('fsdp', 'ctx'))
- grad_fc: float32 [1024, 4096], P(('fsdp', 'ctx'), 'tp')
- grad_fc_bias: float32 [4096], P('tp')
- grad_out: float32 [4096, 1024], P('tp', ('fsdp', 'ctx'))
- grad_out_bias: float32 [1024], P(('fsdp', 'ctx'))
- root_squares: float32 [4], replicated
Inputs may be any that keep to these rules, and one draw needn't show every extreme that they name: `tokens`: each row is a value drawn near zero scaled by a factor that depends on the row. `piece_starts`: piece k of a sequence starts at k * (2048) or later and ends by (k + 1) * 2048; pieces never intersect. `seq_lengths`: some sequence is full in every draw.
All inputs are finite; a program needn't handle non-finite values.
Results may differ from a plain program's by a relative error of at most 0.02.
Values may be sent and summed in bfloat16 or wider, within the bound.
No kernel may reach another device: no remote copies, remote signals or barrier semaphores. Data moves between devices by JAX's collectives and lax.ppermute only.
A program may use at most 128 MiB of HBM per device.

v0:
```python
from functools import partial

import jax
import jax.numpy as jnp
from jax import lax
from jax.sharding import PartitionSpec as P

HEAD = 64
PIECE = 256


NORM_EPS = 1e-05
ROOT_EPS = 1e-06
MASKED = -1e30


def layer_norm(values, gain, shift):
    center = values - jnp.mean(values, axis=-1, keepdims=True)
    spread = jnp.mean(center * center, axis=-1, keepdims=True)
    return center * lax.rsqrt(spread + NORM_EPS) * gain + shift


def gelu_tanh(values):
    return jax.nn.gelu(values, approximate=True)


def piece_number(positions, starts):
    inside = (positions[:, None] >= starts[None, :]) & (
        positions[:, None] < starts[None, :] + PIECE
    )
    labels = jnp.arange(1, starts.shape[0] + 1, dtype=jnp.int32)
    return jnp.sum(jnp.where(inside, labels[None, :], 0), axis=1)


def pieces_for(positions, starts_all):
    return jax.vmap(piece_number, in_axes=(None, 0))(positions, starts_all)


def visible(query_pos, query_piece, key_pos, key_piece, length):
    causal = key_pos[None, :] <= query_pos[:, None]
    shared = (query_piece[:, None] == key_piece[None, :]) & (query_piece[:, None] > 0)
    return (key_pos[None, :] < length) & (causal | shared)


def block_scores(query_heads, key_block, allowed):
    scaled = (
        jnp.einsum("qhe,khe->hqk", query_heads, key_block, preferred_element_type=jnp.float32)
        * 0.125
    )
    return jnp.where(allowed[None], scaled, MASKED)


def split_blocks(array_in, block_rows):
    return array_in.reshape((array_in.shape[0] // block_rows, block_rows) + array_in.shape[1:])


def attend(
    query_heads,
    key_heads,
    value_heads,
    query_pos,
    query_piece,
    key_pos,
    key_piece,
    length,
    block_rows,
):
    heads_here = query_heads.shape[1]
    local_rows = query_heads.shape[0]
    key_blocks = split_blocks(key_heads, block_rows)
    pos_blocks = split_blocks(key_pos, block_rows)
    piece_blocks = split_blocks(key_piece, block_rows)

    def first_pass(state_pair, block_items):
        running_max, running_sum = state_pair
        key_block, key_block_pos, key_block_piece = block_items
        allowed = visible(query_pos, query_piece, key_block_pos, key_block_piece, length)
        scores = block_scores(query_heads, key_block, allowed)
        new_max = jnp.maximum(running_max, jnp.max(scores, axis=2))
        kept_terms = jnp.where(allowed[None], jnp.exp(scores - new_max[..., None]), 0.0)
        return (
            (new_max, running_sum * jnp.exp(running_max - new_max) + jnp.sum(kept_terms, axis=2)),
            None,
        )

    start_state = (
        jnp.full((heads_here, local_rows), MASKED, jnp.float32),
        jnp.zeros((heads_here, local_rows), jnp.float32),
    )
    (row_max, row_sum), _ = lax.scan(
        first_pass, start_state, (key_blocks, pos_blocks, piece_blocks)
    )
    log_sum = row_max + jnp.log(row_sum)

    def second_pass(accumulated, block_items):
        key_block, value_block, key_block_pos, key_block_piece = block_items
        allowed = visible(query_pos, query_piece, key_block_pos, key_block_piece, length)
        scores = block_scores(query_heads, key_block, allowed)
        attn_probs = jnp.where(allowed[None], jnp.exp(scores - log_sum[..., None]), 0.0).astype(
            jnp.bfloat16
        )
        return (
            accumulated
            + jnp.einsum(
                "hqk,khe->qhe", attn_probs, value_block, preferred_element_type=jnp.float32
            ),
            None,
        )

    outputs, _ = lax.scan(
        second_pass,
        jnp.zeros((local_rows, heads_here, HEAD), jnp.float32),
        (key_blocks, split_blocks(value_heads, block_rows), pos_blocks, piece_blocks),
    )
    return (outputs, log_sum)


def query_side(
    query_heads,
    grad_heads,
    log_sum,
    delta_rows,
    key_heads,
    value_heads,
    query_pos,
    query_piece,
    key_pos,
    key_piece,
    length,
    block_rows,
    with_keys,
):

    def key_step(grad_query, block_items):
        key_block, value_block, key_block_pos, key_block_piece = block_items
        allowed = visible(query_pos, query_piece, key_block_pos, key_block_piece, length)
        scores = block_scores(query_heads, key_block, allowed)
        attn_probs = jnp.where(allowed[None], jnp.exp(scores - log_sum[..., None]), 0.0)
        grad_probs = jnp.einsum(
            "qhe,khe->hqk", grad_heads, value_block, preferred_element_type=jnp.float32
        )
        grad_scores = (0.125 * attn_probs * (grad_probs - delta_rows[..., None])).astype(
            jnp.bfloat16
        )
        grad_query = grad_query + jnp.einsum(
            "hqk,khe->qhe", grad_scores, key_block, preferred_element_type=jnp.float32
        )
        grad_key = jnp.einsum(
            "hqk,qhe->khe", grad_scores, query_heads, preferred_element_type=jnp.float32
        )
        grad_value = jnp.einsum(
            "hqk,qhe->khe",
            attn_probs.astype(jnp.bfloat16),
            grad_heads,
            preferred_element_type=jnp.float32,
        )
        return (grad_query, (grad_key, grad_value))

    block_items = (
        split_blocks(key_heads, block_rows),
        split_blocks(value_heads, block_rows),
        split_blocks(key_pos, block_rows),
        split_blocks(key_piece, block_rows),
    )
    return lax.scan(key_step, jnp.zeros(query_heads.shape, jnp.float32), block_items)


def column_sums(field):
    return jnp.sum(field.astype(jnp.float32), axis=0)


def body(
    tokens,
    ln1_gain,
    ln1_bias,
    qkv_weight,
    qv_bias,
    proj_weight,
    proj_bias,
    ln2_gain,
    ln2_bias,
    fc_weight,
    fc_bias,
    out_weight,
    out_bias,
    piece_starts,
    seq_lengths,
    cotangent,
):
    seq_here = tokens.shape[0]
    local_rows = tokens.shape[1]
    width = tokens.shape[2]
    all_rows = seq_here * local_rows
    own_lengths = lax.dynamic_slice_in_dim(
        seq_lengths, lax.axis_index("fsdp") * seq_here, seq_here, 0
    )
    gain_one, shift_one, w_qkv, w_proj, b_proj = (
        lax.all_gather(ln1_gain, ("fsdp", "ctx"), axis=0, tiled=True),
        lax.all_gather(ln1_bias, ("fsdp", "ctx"), axis=0, tiled=True),
        lax.all_gather(qkv_weight, ("fsdp", "ctx"), axis=0, tiled=True),
        lax.all_gather(proj_weight, ("fsdp", "ctx"), axis=1, tiled=True),
        lax.all_gather(proj_bias, ("fsdp", "ctx"), axis=0, tiled=True),
    )
    head_cols = w_qkv.shape[2]
    heads_here = head_cols // HEAD
    full_length = local_rows * lax.axis_size("ctx")
    block_rows = min(512, full_length)
    query_pos = lax.axis_index("ctx") * local_rows + jnp.arange(local_rows, dtype=jnp.int32)
    key_pos = jnp.arange(full_length, dtype=jnp.int32)
    query_piece = pieces_for(query_pos, piece_starts)
    key_piece = pieces_for(key_pos, piece_starts)
    valid_rows = (query_pos[None, :] < own_lengths[:, None]).reshape(all_rows).astype(jnp.float32)
    inputs = tokens.astype(jnp.float32).reshape(all_rows, width)
    normed_f, norm_one_back = jax.vjp(
        layer_norm, inputs, gain_one.astype(jnp.float32), shift_one.astype(jnp.float32)
    )
    normed = normed_f.astype(jnp.bfloat16)
    project = jnp.einsum("td,dcn->tcn", normed, w_qkv, preferred_element_type=jnp.float32)
    bias_pair = qv_bias.astype(jnp.float32)
    query_flat = (
        (project[:, 0] + bias_pair[0]).astype(jnp.bfloat16).reshape(seq_here, local_rows, head_cols)
    )
    key_flat = project[:, 1].astype(jnp.bfloat16).reshape(seq_here, local_rows, head_cols)
    value_flat = (
        (project[:, 2] + bias_pair[1]).astype(jnp.bfloat16).reshape(seq_here, local_rows, head_cols)
    )
    key_all, value_all = (
        lax.all_gather(key_flat, "ctx", axis=1, tiled=True),
        lax.all_gather(value_flat, "ctx", axis=1, tiled=True),
    )
    query_heads = query_flat.reshape(seq_here, local_rows, heads_here, HEAD)
    key_heads = key_all.reshape(seq_here, full_length, heads_here, HEAD)
    value_heads = value_all.reshape(seq_here, full_length, heads_here, HEAD)
    attend_all = jax.vmap(
        partial(attend, block_rows=block_rows), in_axes=(0, 0, 0, None, 0, None, 0, 0)
    )
    attended, log_sum = attend_all(
        query_heads, key_heads, value_heads, query_pos, query_piece, key_pos, key_piece, own_lengths
    )
    heads_out = attended.reshape(all_rows, head_cols).astype(jnp.bfloat16)
    attn_out = lax.psum(
        jnp.dot(heads_out, w_proj, preferred_element_type=jnp.float32).astype(jnp.bfloat16), "tp"
    ).astype(jnp.float32) + b_proj.astype(jnp.float32)
    middle = inputs + attn_out
    gain_two, shift_two, w_fc, w_out, b_out = (
        lax.all_gather(ln2_gain, ("fsdp", "ctx"), axis=0, tiled=True),
        lax.all_gather(ln2_bias, ("fsdp", "ctx"), axis=0, tiled=True),
        lax.all_gather(fc_weight, ("fsdp", "ctx"), axis=0, tiled=True),
        lax.all_gather(out_weight, ("fsdp", "ctx"), axis=1, tiled=True),
        lax.all_gather(out_bias, ("fsdp", "ctx"), axis=0, tiled=True),
    )
    normed_two_f, norm_two_back = jax.vjp(
        layer_norm, middle, gain_two.astype(jnp.float32), shift_two.astype(jnp.float32)
    )
    normed_two = normed_two_f.astype(jnp.bfloat16)
    hidden = jnp.dot(normed_two, w_fc, preferred_element_type=jnp.float32) + fc_bias.astype(
        jnp.float32
    )
    activated_f, gelu_back = jax.vjp(gelu_tanh, hidden)
    activated = activated_f.astype(jnp.bfloat16)
    mlp_out = lax.psum(
        jnp.dot(activated, w_out, preferred_element_type=jnp.float32).astype(jnp.bfloat16), "tp"
    ).astype(jnp.float32) + b_out.astype(jnp.float32)
    final = middle + mlp_out
    grad_final = cotangent.astype(jnp.float32).reshape(all_rows, width) * valid_rows[:, None]
    grad_mlp = grad_final.astype(jnp.bfloat16)
    grad_out_bias = column_sums(grad_mlp)
    grad_out = jnp.einsum("tf,td->fd", activated, grad_mlp, preferred_element_type=jnp.float32)
    grad_act = jnp.einsum("td,fd->tf", grad_mlp, w_out, preferred_element_type=jnp.float32)
    grad_hidden = gelu_back(grad_act)[0].astype(jnp.bfloat16)
    grad_fc_part = column_sums(grad_hidden)
    grad_fc = jnp.einsum("td,tf->df", normed_two, grad_hidden, preferred_element_type=jnp.float32)
    grad_norm_two = lax.psum(
        jnp.einsum("tf,df->td", grad_hidden, w_fc, preferred_element_type=jnp.float32).astype(
            jnp.bfloat16
        ),
        "tp",
    ).astype(jnp.float32)
    middle_part, grad_ln2_gain, grad_ln2_bias = norm_two_back(grad_norm_two)
    grad_middle = grad_final + middle_part
    grad_ln2_gain, grad_ln2_bias, grad_fc, grad_out, grad_out_bias = (
        lax.psum_scatter(grad_ln2_gain, ("fsdp", "ctx"), scatter_dimension=0, tiled=True),
        lax.psum_scatter(grad_ln2_bias, ("fsdp", "ctx"), scatter_dimension=0, tiled=True),
        lax.psum_scatter(grad_fc, ("fsdp", "ctx"), scatter_dimension=0, tiled=True),
        lax.psum_scatter(grad_out, ("fsdp", "ctx"), scatter_dimension=1, tiled=True),
        lax.psum_scatter(grad_out_bias, ("fsdp", "ctx"), scatter_dimension=0, tiled=True),
    )
    grad_attn = grad_middle.astype(jnp.bfloat16)
    grad_proj_bias = column_sums(grad_attn)
    grad_proj = jnp.einsum("tn,td->nd", heads_out, grad_attn, preferred_element_type=jnp.float32)
    grad_flat = (
        jnp.einsum("td,nd->tn", grad_attn, w_proj, preferred_element_type=jnp.float32)
        .astype(jnp.bfloat16)
        .reshape(seq_here, local_rows, head_cols)
    )
    grad_heads = grad_flat.reshape(seq_here, local_rows, heads_here, HEAD)
    delta_rows = jnp.einsum("sqhe,sqhe->shq", grad_heads.astype(jnp.float32), attended)
    query_all_side = jax.vmap(
        partial(query_side, block_rows=block_rows, with_keys=True),
        in_axes=(0, 0, 0, 0, 0, 0, None, 0, None, 0, 0),
    )
    grad_query, key_terms = query_all_side(
        query_heads,
        grad_heads,
        log_sum,
        delta_rows,
        key_heads,
        value_heads,
        query_pos,
        query_piece,
        key_pos,
        key_piece,
        own_lengths,
    )
    grad_key, grad_value = (
        lax.psum_scatter(
            key_terms[0].reshape(seq_here, full_length, head_cols).astype(jnp.bfloat16),
            "ctx",
            scatter_dimension=1,
            tiled=True,
        ).astype(jnp.float32),
        lax.psum_scatter(
            key_terms[1].reshape(seq_here, full_length, head_cols).astype(jnp.bfloat16),
            "ctx",
            scatter_dimension=1,
            tiled=True,
        ).astype(jnp.float32),
    )
    grad_query_low = grad_query.reshape(all_rows, head_cols).astype(jnp.bfloat16)
    grad_key_low = grad_key.reshape(all_rows, head_cols).astype(jnp.bfloat16)
    grad_value_low = grad_value.reshape(all_rows, head_cols).astype(jnp.bfloat16)
    grad_project = jnp.stack([grad_query_low, grad_key_low, grad_value_low], axis=1)
    grad_qv_part = jnp.stack([column_sums(grad_query_low), column_sums(grad_value_low)])
    grad_qkv = jnp.einsum("td,tcn->dcn", normed, grad_project, preferred_element_type=jnp.float32)
    grad_normed = lax.psum(
        jnp.einsum("tcn,dcn->td", grad_project, w_qkv, preferred_element_type=jnp.float32).astype(
            jnp.bfloat16
        ),
        "tp",
    ).astype(jnp.float32)
    input_part, grad_ln1_gain, grad_ln1_bias = norm_one_back(grad_normed)
    grad_inputs = grad_middle + input_part
    grad_ln1_gain, grad_ln1_bias, grad_qkv, grad_proj, grad_proj_bias = (
        lax.psum_scatter(grad_ln1_gain, ("fsdp", "ctx"), scatter_dimension=0, tiled=True),
        lax.psum_scatter(grad_ln1_bias, ("fsdp", "ctx"), scatter_dimension=0, tiled=True),
        lax.psum_scatter(grad_qkv, ("fsdp", "ctx"), scatter_dimension=0, tiled=True),
        lax.psum_scatter(grad_proj, ("fsdp", "ctx"), scatter_dimension=1, tiled=True),
        lax.psum_scatter(grad_proj_bias, ("fsdp", "ctx"), scatter_dimension=0, tiled=True),
    )

    def squares(field):
        return jnp.sum(valid_rows * jnp.sum(field * field, axis=1))

    square_sums = jnp.stack([squares(inputs), squares(attn_out), squares(mlp_out), squares(final)])
    square_total, grad_qv_bias, grad_fc_bias = lax.psum(
        (square_sums, grad_qv_part, grad_fc_part), ("fsdp", "ctx")
    )
    valid_total = jnp.sum(seq_lengths).astype(jnp.float32)
    root_squares = jnp.sqrt(square_total / (valid_total * width) + ROOT_EPS)
    layer_out = final.reshape(seq_here, local_rows, width).astype(jnp.bfloat16)
    grad_tokens = grad_inputs.reshape(seq_here, local_rows, width).astype(jnp.bfloat16)
    return (
        layer_out,
        grad_tokens,
        grad_ln1_gain,
        grad_ln1_bias,
        grad_qkv,
        grad_qv_bias,
        grad_proj,
        grad_proj_bias,
        grad_ln2_gain,
        grad_ln2_bias,
        grad_fc,
        grad_fc_bias,
        grad_out,
        grad_out_bias,
        root_squares,
    )


def solution(mesh):
    in_specs = (
        P("fsdp", "ctx", None),
        P(("fsdp", "ctx")),
        P(("fsdp", "ctx")),
        P(("fsdp", "ctx"), None, "tp"),
        P(None, "tp"),
        P("tp", ("fsdp", "ctx")),
        P(("fsdp", "ctx")),
        P(("fsdp", "ctx")),
        P(("fsdp", "ctx")),
        P(("fsdp", "ctx"), "tp"),
        P("tp"),
        P("tp", ("fsdp", "ctx")),
        P(("fsdp", "ctx")),
        P("fsdp", None),
        P(),
        P("fsdp", "ctx", None),
    )
    out_specs = (
        P("fsdp", "ctx", None),
        P("fsdp", "ctx", None),
        P(("fsdp", "ctx")),
        P(("fsdp", "ctx")),
        P(("fsdp", "ctx"), None, "tp"),
        P(None, "tp"),
        P("tp", ("fsdp", "ctx")),
        P(("fsdp", "ctx")),
        P(("fsdp", "ctx")),
        P(("fsdp", "ctx")),
        P(("fsdp", "ctx"), "tp"),
        P("tp"),
        P("tp", ("fsdp", "ctx")),
        P(("fsdp", "ctx")),
        P(),
    )
    return jax.shard_map(body, mesh=mesh, in_specs=in_specs, out_specs=out_specs, check_vma=False)
```

profile of v0, /device:TPU:0, one launch (start us, length us, event | category | flops | bytes accessed | tf_op | source)
XLA Modules:
  0.0 2491.8 jit_solution(14332724150216629482)
XLA Ops:
  15.0 331.3 %all-reduce.13 = (bf16[1024]{0:T(1024)(128)(2,1)S(1)}, bf16[1024]{0:T(1024)(128)(2,1)S(1)}, bf16[1024]{0:T(1024)(128)(2,1)S(1)}, bf16[1024]{0:T(1024)(128)(2,1)S...) all-reduce(bf16[1024]{0:T(1024)(128)(2,1)S(1)} %dynamic-update-slic, ...), channel_id=1, replica_groups=mesh['fsdp'=4,'ctx'=16,'tp'=2] {'fsdp','ctx'}, use_global_device_ids=true, to_apply=%add.4 | all-reduce | flops 6144 | bytes 24576
  348.9 3.1 fusion.121
  356.8 46.8 %all-gather.18.cloned.1.call-done = bf16[4096,1,512]{2,0,1:T(8,128)(2,1)} async-done(((bf16[256,1,512]{2,0,1:T(8,128)(2,1)}), bf16[4096,1,512]{2,0,1:T(8,128)(2,1)}) %all-gather.18.cloned.1.call-update) | async-done | bytes 4194320 | tf_op jit(solution)/shard_map/all_gather | solution.py:228
  403.6 11.2 reshape.1101
  414.7 9.8 copy.95
  424.5 64.8 %while.39 = (s32[]{:T(128)}, f32[1,8,256]{2,1,0:T(8,128)S(1)}, f32[1,8,256]{2,1,0:T(8,128)S(1)}, s32[8,512]{1,0:T(8,128)S(1)}, s32[1]{0:T(128)}, /*index=5*/s32[...) while((s32[]{:T(128)}, f32[1,8,256]{2,1,0:T(8,128)S(1)}, ...), condition=%wide.region_7.8_spmd.clone, body=%wide.region_4.7_spmd.clone.sunk | while | flops 143272960 | bytes 9695376 | solution.py:90
  425.5 3.9 fusion.166
  429.4 3.2 select_reduce_fusion.6
  433.6 3.9 fusion.166
  437.5 3.2 select_reduce_fusion.6
  441.7 3.9 fusion.166
  445.6 3.2 select_reduce_fusion.6
  449.8 3.9 fusion.166
  453.7 3.2 select_reduce_fusion.6
  458.0 3.9 fusion.166
  461.9 3.2 select_reduce_fusion.6
  466.1 3.9 fusion.166
  469.9 3.2 select_reduce_fusion.6
  474.2 3.9 fusion.166
  478.0 3.2 select_reduce_fusion.6
  482.3 3.9 fusion.166
  486.1 3.2 select_reduce_fusion.6
  489.4 11.2 reshape.1100
  500.5 9.8 copy.94
  510.3 31.0 %while.40 = (s32[]{:T(128)}, f32[1,256,8,64]{1,3,2,0:T(8,128)S(1)}, bf16[8,1,512,8,64]{2,4,3,1,0:T(8,128)(2,1)}, s32[8,512]{1,0:T(8,128)S(1)}, s32[1]{0:T(128)},...) while((s32[]{:T(128)}, f32[1,256,8,64]{1,3,2,0:T(8,128)S(1)}, ...), condition=%wide.region_9.10_spmd.clone, body=%wide.region_8.9_spmd.clone.sunk | while | flops 274596864 | bytes 2650775 | solution.py:110
  546.7 31.7 %all-reduce.19.cloned.1.call-done = bf16[256,1024]{1,0:T(8,128)(2,1)} async-done(((bf16[256,1024]{1,0:T(8,128)(2,1)}), bf16[256,1024]{1,0:T(8,128)(2,1)}) %all-reduce.19.cloned.1.call-update) | async-done | bytes 524304 | tf_op jit(solution)/shard_map/psum | solution.py:241
  581.1 75.2 %all-gather.14.cloned.1.call-done = bf16[1024,2048]{1,0:T(8,128)(2,1)} async-done(((bf16[16,2048]{1,0:T(8,128)(2,1)}), bf16[1024,2048]{1,0:T(8,128)(2,1)}) %all-gather.14.cloned.1.call-update) | async-done | bytes 4194320 | tf_op jit(solution)/shard_map/all_gather | solution.py:248
  656.3 5.1 convolution_add_fusion
  661.5 68.7 %all-gather.16.cloned.1.call-done = bf16[2048,1024]{0,1:T(8,128)(2,1)} async-done(((bf16[2048,16]{0,1:T(8,128)(2,1)}), bf16[2048,1024]{0,1:T(8,128)(2,1)}) %all-gather.16.cloned.1.call-update) | async-done | bytes 4194320 | tf_op jit(solution)/shard_map/all_gather | solution.py:249
  730.1 5.2 convolution_convert_fusion.2
  741.3 43.5 %all-reduce.23.cloned.1.call-done = (bf16[256,1024]{1,0:T(8,128)(2,1)}, bf16[256,1024]{1,0:T(8,128)(2,1)}) async-done(((bf16[256,1024]{1,0:T(8,128)(2,1)}, bf16[256,1024]{1,0:T(8,128)(2,1)}), (bf16[256,1024]{1,0:T(8,128)(2,1)}, bf16[256,1024]{1,0:T(8,128)(2,1)})) %all-reduce.23.cloned.1.call-update) | async-done | bytes 1048592 | tf_op jit(solution)/shard_map/psum | solution.py:261
  793.8 101.5 %while.41 = (s32[]{:T(128)}, f32[1,256,8,64]{1,3,2,0:T(8,128)}, bf16[8,1,512,8,64]{2,4,3,1,0:T(8,128)(2,1)}, bf16[8,1,512,8,64]{2,4,3,1,0:T(8,128)(2,1)}, bf16[8...) while((s32[]{:T(128)}, f32[1,256,8,64]{1,3,2,0:T(8,128)}, ...), condition=%wide.region_18.19_spmd.clone, body=%wide.region_17.18_spmd.clone.sunk | while | flops 685638656 | bytes 25082040 | solution.py:165
  838.9 3.1 fusion.185
  895.2 10.0 copy.119
  905.2 11.8 reshape.1092
  917.1 10.0 copy.120
  927.1 12.0 reshape.1093
  940.5 58.2 %reduce-scatter.7.cloned.1.call-done = bf16[1,256,512]{2,1,0:T(8,128)(2,1)} async-done(((bf16[1,4096,512]{2,1,0:T(8,128)(2,1)}), bf16[1,256,512]{2,1,0:T(8,128)(2,1)}) %reduce-scatter.7.cloned.1.call-update) | async-done | bytes 262160 | tf_op jit(solution)/shard_map/reduce_scatter | solution.py:316
  998.7 83.4 %reduce-scatter.9.cloned.1.call-done = bf16[1,256,512]{2,1,0:T(8,128)(2,1)} async-done(((bf16[1,4096,512]{2,1,0:T(8,128)(2,1)}), bf16[1,256,512]{2,1,0:T(8,128)(2,1)}) %reduce-scatter.9.cloned.1.call-update) | async-done | bytes 262160 | tf_op jit(solution)/shard_map/reduce_scatter | solution.py:322
  1082.1 3.9 fusion.79
  1088.2 4.8 fusion.119
  1094.0 6.3 fusion.113
  1101.4 3.9 fusion.106
  1111.3 8.6 all-reduce.21.cloned.1.call-done
  1123.0 329.6 %all-reduce.12 = (f32[1024]{0:T(1024)S(1)}, f32[1024]{0:T(1024)S(1)}, f32[2,512]{1,0:T(2,128)}, f32[1024]{0:T(1024)S(1)}, f32[1024]{0:T(1024)S(1)}, /*index=5*/f...) all-reduce(f32[1024]{0:T(1024)S(1)} %get-tuple-element.484, ...), channel_id=5, replica_groups=mesh['fsdp'=4,'ctx'=16,'tp'=2] {'fsdp','ctx'}, use_global_device_ids=true, to_apply=%region_25.26.clone | all-reduce | flops 9220 | bytes 73760
  1459.4 343.1 %reduce-scatter.15.cloned.1.call-done = f32[16,2048]{1,0:T(8,128)} async-done(((f32[1024,2048]{1,0:T(8,128)}), f32[16,2048]{1,0:T(8,128)}) %reduce-scatter.15.cloned.1.call-update) | async-done | bytes 131088 | tf_op jit(solution)/shard_map/reduce_scatter | solution.py:284
  1802.5 343.4 %reduce-scatter.17.cloned.1.call-done = f32[2048,16]{0,1:T(8,128)} async-done(((f32[2048,1024]{0,1:T(8,128)}), f32[2048,16]{0,1:T(8,128)}) %reduce-scatter.17.cloned.1.call-update) | async-done | bytes 131088 | tf_op jit(solution)/shard_map/reduce_scatter | solution.py:285
  2146.0 338.9 %reduce-scatter.11.cloned.1.call-done = f32[16,3,512]{2,0,1:T(8,128)} async-done(((f32[1024,3,512]{2,0,1:T(8,128)}), f32[16,3,512]{2,0,1:T(8,128)}) %reduce-scatter.11.cloned.1.call-update) | async-done | bytes 98320 | tf_op jit(solution)/shard_map/reduce_scatter | solution.py:346
  (383 shorter events, 193.4 us)
Async XLA Ops:
  7.2 345.8 %copy-start.17 = (bf16[2,512]{1,0:T(2,128)(2,1)S(1)}, bf16[2,512]{1,0:T(2,128)(2,1)}, u32[]{:S(2)}) copy-start(bf16[2,512]{1,0:T(2,128)(2,1)} %param.26) | copy-start | bytes 6148
  7.2 341.7 %all-gather.8.cloned.1.call-start = ((), (), s32[]{:S(2)}) async-start(), calls=%async_computation.6 | async-start | bytes 3194880 | tf_op jit(solution)/shard_map/all_gather | solution.py:200
  7.9 395.7 %all-gather.18.cloned.1.call-start = ((), (), s32[]{:S(2)}) async-start(), calls=%async_computation.19 | async-start | bytes 4456448 | tf_op jit(solution)/shard_map/all_gather | solution.py:228
  348.8 5.7 copy-start.19
  348.8 5.9 copy-start.23
  352.0 2.7 copy-start.12
  352.9 136.5 %all-gather.10.cloned.1.call-start = ((), (), s32[]{:S(2)}) async-start(), calls=%async_computation.7 | async-start | bytes 4456448 | tf_op jit(solution)/shard_map/all_gather | solution.py:229
  353.7 187.6 %all-gather.12.cloned.1.call-start = ((), (), s32[]{:S(2)}) async-start(), calls=%async_computation.8 | async-start | bytes 1064960 | tf_op jit(solution)/shard_map/all_gather | solution.py:201
  354.3 224.1 %all-reduce.19.cloned.1.call-start = ((), (), s32[]{:S(2)}) async-start(), calls=%async_computation.9 | async-start | bytes 1048576 | tf_op jit(solution)/shard_map/psum | solution.py:241
  510.3 35.2 %copy-start.18 = (bf16[2048]{0:T(1024)(128)(2,1)S(1)}, bf16[2048]{0:T(1024)(128)(2,1)}, u32[]{:S(2)}) copy-start(bf16[2048]{0:T(1024)(128)(2,1)} %param.32) | copy-start | bytes 12292
  510.3 68.1 %copy-start = (bf16[1,256,1024]{2,1,0:T(8,128)(2,1)S(1)}, bf16[1,256,1024]{2,1,0:T(8,128)(2,1)}, u32[]{:S(2)}) copy-start(bf16[1,256,1024]{2,1,0:T(8,128)(2,1)} %param.22) | copy-start | bytes 1572868
  541.3 120.1 %copy-start.10 = (bf16[1,256,8,64]{1,3,2,0:T(8,128)(2,1)}, bf16[1,256,8,64]{1,3,2,0:T(8,128)(2,1)S(1)}, u32[]{:S(2)}) copy-start(bf16[1,256,8,64]{1,3,2,0:T(8,128)(2,1)S(1)} %convert_element_type.237) | copy-start | bytes 786436
  544.0 112.4 %all-gather.14.cloned.1.call-start = ((), (), s32[]{:S(2)}) async-start(), calls=%async_computation.10 | async-start | bytes 4259840 | tf_op jit(solution)/shard_map/all_gather | solution.py:248
  544.6 185.6 %all-gather.16.cloned.1.call-start = ((), (), s32[]{:S(2)}) async-start(), calls=%async_computation.11 | async-start | bytes 4259840 | tf_op jit(solution)/shard_map/all_gather | solution.py:249
  545.3 239.6 %all-reduce.23.cloned.1.call-start = ((), (), s32[]{:S(2)}) async-start(), calls=%async_computation.20 | async-start | bytes 2097152 | tf_op jit(solution)/shard_map/psum | solution.py:261
  661.5 73.9 %copy-start.5 = (bf16[1,256,1024]{2,1,0:T(8,128)(2,1)S(1)}, bf16[1,256,1024]{2,1,0:T(8,128)(2,1)}, u32[]{:S(2)}) copy-start(bf16[1,256,1024]{2,1,0:T(8,128)(2,1)} %param.37) | copy-start | bytes 1572868
  730.1 5.2 copy-start.9
  730.1 5.2 copy-start.22
  735.4 3.4 copy-start.21
  737.8 1.0 copy-start.13
  738.8 46.1 %copy-start.1 = (bf16[256,1024]{1,0:T(8,128)(2,1)S(1)}, bf16[256,1024]{1,0:T(8,128)(2,1)}, u32[]{:S(2)}) copy-start(bf16[256,1024]{1,0:T(8,128)(2,1)} %all-reduce.19.cloned.1.call-done) | copy-start | bytes 1572868
  741.0 257.7 %reduce-scatter.7.cloned.1.call-start = ((), (), s32[]{:S(2)}) async-start(), calls=%async_computation.12 | async-start | bytes 4456448 | tf_op jit(solution)/shard_map/reduce_scatter | solution.py:316
  784.9 4.5 copy-start.3
  790.0 3.7 copy-start.7
  917.1 165.1 %reduce-scatter.9.cloned.1.call-start = ((), (), s32[]{:S(2)}) async-start(), calls=%async_computation.13 | async-start | bytes 4456448 | tf_op jit(solution)/shard_map/reduce_scatter | solution.py:322
  939.1 1.1 copy-start.2
  939.1 146.9 %copy-start.8 = (bf16[256,1024]{1,0:T(8,128)(2,1)S(1)}, bf16[256,1024]{1,0:T(8,128)(2,1)}, u32[]{:S(2)}) copy-start(bf16[256,1024]{1,0:T(8,128)(2,1)} %copy-done.7) | copy-start | bytes 1572868
  939.2 146.9 %copy-start.11 = (bf16[1,256,8,64]{1,3,2,0:T(8,128)(2,1)S(1)}, bf16[1,256,8,64]{1,3,2,0:T(8,128)(2,1)}, u32[]{:S(2)}) copy-start(bf16[1,256,8,64]{1,3,2,0:T(8,128)(2,1)} %copy-done.10) | copy-start | bytes 786436
  939.2 180.7 %all-reduce.21.cloned.1.call-start = ((), (), s32[]{:S(2)}) async-start(), calls=%async_computation.14 | async-start | bytes 1048576 | tf_op jit(solution)/shard_map/psum | solution.py:335
  1086.0 2.3 copy-start.14
  1086.0 373.4 %reduce-scatter.13.cloned.1.call-start = ((), (), s32[]{:S(2)}) async-start(), calls=%async_computation.16 | async-start | bytes 2129920 | tf_op jit(solution)/shard_map/reduce_scatter | solution.py:347
  1087.9 714.6 %reduce-scatter.15.cloned.1.call-start = ((), (), s32[]{:S(2)}) async-start(), calls=%async_computation.17 | async-start | bytes 8519680 | tf_op jit(solution)/shard_map/reduce_scatter | solution.py:284
  1093.0 1.0 copy-start.6
  1093.0 1052.9 %reduce-scatter.17.cloned.1.call-start = ((), (), s32[]{:S(2)}) async-start(), calls=%async_computation.18 | async-start | bytes 8519680 | tf_op jit(solution)/shard_map/reduce_scatter | solution.py:285
  1100.4 1.0 copy-start.15
  1100.4 1.0 copy-start.16
  1100.4 1384.5 %reduce-scatter.11.cloned.1.call-start = ((), (), s32[]{:S(2)}) async-start(), calls=%async_computation.15 | async-start | bytes 6389760 | tf_op jit(solution)/shard_map/reduce_scatter | solution.py:346
  1105.3 0.7 copy-start.24
  1105.3 2.7 copy-start.20
  1105.3 351.4 %copy-start.4 = (bf16[256,1024]{1,0:T(8,128)(2,1)S(1)}, bf16[256,1024]{1,0:T(8,128)(2,1)}, u32[]{:S(2)}) copy-start(bf16[256,1024]{1,0:T(8,128)(2,1)} %get-tuple-element.584) | copy-start | bytes 1572868
Sparse Core Ops, SparseCore 0:
  11.3 73.8 all-gather.7
  353.0 50.5 all-gather.17
  406.6 54.7 all-gather.9
  464.4 64.7 all-gather.11
  544.1 34.2 all-reduce.18
  582.0 74.2 all-gather.13
  660.1 70.0 all-gather.15
  741.1 43.6 all-reduce.22
  917.2 81.5 reduce-scatter.6
  1003.2 78.8 reduce-scatter.8
  1086.1 33.7 all-reduce.20
  1122.8 336.2 reduce-scatter.12
  1462.0 340.4 reduce-scatter.14
  1805.4 340.5 reduce-scatter.16
  2148.8 336.0 reduce-scatter.10
where the time goes:
time: 2500 us; the launch traced here: 2490 us
  waiting for transfers between devices  1440 us (58%)
  blocking collectives  661 us (26%)
  matrix products  190 us (8%)
  local copies, waits for them, and re-layouts  104 us (4%)
  other arithmetic  72.3 us (3%)
    unnamed x2, blocking collectives  661 us
    reduce_scatter x1, waiting for transfers between devices, body(): lax.psum_scatter(grad_out, ('fsdp', 'ctx'), scatter_dimension=1, tiled=True)  343 us
    reduce_scatter x1, waiting for transfers between devices, body(): lax.psum_scatter(grad_fc, ('fsdp', 'ctx'), scatter_dimension=0, tiled=True)  343 us
    reduce_scatter x1, waiting for transfers between devices, body(): lax.psum_scatter(grad_qkv, ('fsdp', 'ctx'), scatter_dimension=0, tiled=True)  339 us
    reduce_scatter x1, waiting for transfers between devices, body(): lax.psum_scatter(key_terms[1].reshape(seq_here, full_length, head_cols).a...  83.4 us
    all_gather x1, waiting for transfers between devices, body(): lax.all_gather(fc_weight, ('fsdp', 'ctx'), axis=0, tiled=True)  75.2 us
    all_gather x1, waiting for transfers between devices, body(): lax.all_gather(out_weight, ('fsdp', 'ctx'), axis=1, tiled=True)  68.7 us
    reduce_scatter x1, waiting for transfers between devices, body(): lax.psum_scatter(key_terms[0].reshape(seq_here, full_length, head_cols).a...  58.2 us
  transfers between devices with their start and end apart: 15, of which 11 were waited for; matrix products, arithmetic and copies ran while one was open for 8% of the time, Pallas kernels for 0%

commit v1 on v0

v1 whole, which is shorter than its diff:
```python
import jax
import jax.numpy as jnp
from jax import lax
from jax.experimental import pallas as pl
from jax.experimental.pallas import tpu as pltpu
from jax.sharding import Mesh
from jax.sharding import PartitionSpec as P

f32 = jnp.float32
bf16 = jnp.bfloat16
NORM_EPS = 1e-05
ROOT_EPS = 1e-06
B=256; E=64; NB=16; MASKED=-1e30; PIECE=256

def piece_of(pos, info_ref):
    n0=(pos>=info_ref[2])&(pos<info_ref[2]+PIECE)
    n1=(pos>=info_ref[3])&(pos<info_ref[3]+PIECE)
    return jnp.where(n0,1,0)+jnp.where(n1,2,0)

def allowed_block(key_block, query_block, info_ref):
    kpos=key_block*B+lax.broadcasted_iota(jnp.int32,(B,1),0)
    qpos=query_block*B+lax.broadcasted_iota(jnp.int32,(1,B),1)
    kp=piece_of(kpos,info_ref); qp=piece_of(qpos,info_ref)
    qp=jnp.where(qp==0,-1,qp)
    kp=jnp.where(kpos<info_ref[1],kp,-2)
    kpos=jnp.where(kpos<info_ref[1],kpos,1<<20)
    return (kpos<=qpos)|(kp==qp)

def extra_blocks(p, info_ref):
    edge=(2*p+2)*B
    crosses=((info_ref[2]<edge)&(edge<info_ref[2]+PIECE))|((info_ref[3]<edge)&(edge<info_ref[3]+PIECE))
    return jnp.where((info_ref[0]==1)&(p<NB//2-1)&crosses,1,0)

def dot(a,b): return jnp.dot(a,b,preferred_element_type=f32)

def forward_kernel(info_ref, own_ref, other_ref, out_ref, low_ref, lse_ref, key_ref, value_ref):
    core=info_ref[0]
    def stage(p,_):
        key_ref[2*p+core]=own_ref[p,E:2*E,:].T
        value_ref[2*p+core]=own_ref[p,2*E:,:]
        key_ref[2*p+1-core]=other_ref[p,:E,:].T
        value_ref[2*p+1-core]=other_ref[p,E:,:]
        return 0
    lax.fori_loop(0,NB//2,stage,0)
    def one(p,_):
        query=own_ref[p,:E,:]*jnp.asarray(0.125,bf16)
        qb=2*p+core
        def step(blocks,masked,carry):
            top,total,acc=carry
            scores=[dot(key_ref[j],query) for j in blocks]
            if masked: scores=[jnp.where(allowed_block(j,qb,info_ref),s,MASKED) for j,s in zip(blocks,scores)]
            new=top
            for s in scores: new=jnp.maximum(new,jnp.max(s,axis=0,keepdims=True))
            scale=jnp.exp(top-new)
            total=total*scale; acc=acc*scale
            for j,s in zip(blocks,scores):
                e=jnp.exp(s-new)
                total=total+jnp.sum(e,axis=0,keepdims=True)
                acc=acc+dot(value_ref[j],e.astype(bf16))
            return new,total,acc
        carry=(jnp.full((1,B),MASKED,f32),jnp.zeros((1,B),f32),jnp.zeros((E,B),f32))
        carry=step((2*p,2*p+1),True,carry)
        carry=lax.fori_loop(0,p,lambda i,c: step((2*i,2*i+1),False,c),carry)
        carry=lax.fori_loop(0,extra_blocks(p,info_ref),lambda i,c: step((2*p+2,),True,c),carry)
        top,total,acc=carry
        o=acc/total
        out_ref[p]=o
        low_ref[p]=o.astype(bf16)
        lse_ref[p]=top+jnp.log(total)
        return 0
    lax.fori_loop(0,NB//2,one,0)

def backward_kernel(info_ref, own_ref, other_ref, gout_ref, out_ref, lse_ref, gq_ref, gown_ref, gother_ref,
                    key_ref, keyt_ref, value_ref, gk_ref, gv_ref):
    core=info_ref[0]
    def stage(p,_):
        a=own_ref[p,E:2*E,:]; b=other_ref[p,:E,:]
        keyt_ref[2*p+core]=a; keyt_ref[2*p+1-core]=b
        key_ref[2*p+core]=a.T; key_ref[2*p+1-core]=b.T
        value_ref[2*p+core]=own_ref[p,2*E:,:].T
        value_ref[2*p+1-core]=other_ref[p,E:,:].T
        return 0
    lax.fori_loop(0,NB//2,stage,0)
    gk_ref[...]=jnp.zeros_like(gk_ref); gv_ref[...]=jnp.zeros_like(gv_ref)
    def one(p,_):
        query=own_ref[p,:E,:]*jnp.asarray(0.125,bf16)
        rows=query.T
        gout=gout_ref[p]; gout_rows=gout.T
        lse=lse_ref[p]
        delta=jnp.sum(gout.astype(f32)*out_ref[p],axis=0,keepdims=True)
        qb=2*p+core
        def step(blocks,masked,acc):
            for j in blocks:
                s=dot(key_ref[j],query)
                if masked: s=jnp.where(allowed_block(j,qb,info_ref),s,MASKED)
                e=jnp.exp(s-lse)
                gp=dot(value_ref[j],gout)
                gs=(e*(gp-delta)).astype(bf16)
                gv_ref[j]+=dot(e.astype(bf16),gout_rows)
                gk_ref[j]+=dot(gs,rows)
                acc=acc+dot(keyt_ref[j],gs)
            return acc
        acc=step((2*p,2*p+1),True,jnp.zeros((E,B),f32))
        acc=lax.fori_loop(0,p,lambda i,c: step((2*i,2*i+1),False,c),acc)
        acc=lax.fori_loop(0,extra_blocks(p,info_ref),lambda i,c: step((2*p+2,),True,c),acc)
        gq_ref[p]=(acc*0.125).astype(bf16)
        return 0
    lax.fori_loop(0,NB//2,one,0)
    def finish(p,_):
        gown_ref[p,:E,:]=gk_ref[2*p+core].T
        gown_ref[p,E:,:]=gv_ref[2*p+core].T
        gother_ref[p,:E,:]=gk_ref[2*p+1-core].T.astype(bf16)
        gother_ref[p,E:,:]=gv_ref[2*p+1-core].T.astype(bf16)
        return 0
    lax.fori_loop(0,NB//2,finish,0)

VM=pl.BlockSpec(memory_space=pltpu.VMEM); SM=pl.BlockSpec(memory_space=pltpu.SMEM)
LIMIT=48*1024*1024
def attn_forward(info,own,other):
    H=NB//2
    return pl.pallas_call(forward_kernel,
        out_shape=(jax.ShapeDtypeStruct((H,E,B),f32),jax.ShapeDtypeStruct((H,E,B),bf16),jax.ShapeDtypeStruct((H,1,B),f32)),
        in_specs=[SM,VM,VM],out_specs=(VM,VM,VM),
        scratch_shapes=[pltpu.VMEM((NB,B,E),bf16),pltpu.VMEM((NB,E,B),bf16)],
        compiler_params=pltpu.CompilerParams(vmem_limit_bytes=LIMIT),
        cost_estimate=pl.CostEstimate(flops=2*2*B*B*E*72,bytes_accessed=3<<20,transcendentals=B*B*72),
        name="attention_forward")(info,own,other)
def attn_backward(info,own,other,gout,out,lse):
    H=NB//2
    return pl.pallas_call(backward_kernel,
        out_shape=(jax.ShapeDtypeStruct((H,E,B),bf16),jax.ShapeDtypeStruct((H,2*E,B),f32),jax.ShapeDtypeStruct((H,2*E,B),bf16)),
        in_specs=[SM]+[VM]*5,out_specs=(VM,VM,VM),
        scratch_shapes=[pltpu.VMEM((NB,B,E),bf16),pltpu.VMEM((NB,E,B),bf16),pltpu.VMEM((NB,B,E),bf16),pltpu.VMEM((NB,B,E),f32),pltpu.VMEM((NB,B,E),f32)],
        compiler_params=pltpu.CompilerParams(vmem_limit_bytes=LIMIT),
        cost_estimate=pl.CostEstimate(flops=5*2*B*B*E*72,bytes_accessed=5<<20,transcendentals=B*B*72),
        name="attention_backward")(info,own,other,gout,out,lse)


CORE = ("c",)
SPREAD = ("x", "zh", "y")
LINE = ("zh", "y")


def low(field):
    return field.astype(bf16)


def swap(field, axis):
    return lax.ppermute(field, axis, [(0, 1), (1, 0)])


def exchange(field, axes):
    return lax.all_to_all(field, axes, split_axis=0, concat_axis=0, tiled=True)


def spread_out(field):
    return exchange(jnp.broadcast_to(field[None], (32,) + field.shape), SPREAD)


def after(field, *others):
    return lax.optimization_barrier((field, *others))[0]


def contract(a, b, dim_a, dim_b):
    return lax.dot_general(a, b, (((dim_a,), (dim_b,)), ((), ())), preferred_element_type=f32)


def feature_order(core):
    place = jnp.arange(1024, dtype=jnp.int32)
    half = place // 512
    group = (place % 512) // 16
    feature = (group * 2 + jnp.where(half == 0, core, 1 - core)) * 16 + place % 16
    return low(jnp.arange(1024, dtype=jnp.int32)[:, None] == feature[None, :])


def norm_parts(values):
    center = values - jnp.mean(values, axis=-1, keepdims=True)
    inverse = lax.rsqrt(jnp.mean(center * center, axis=-1, keepdims=True) + NORM_EPS)
    return center * inverse, inverse


def norm_back(grad, gain, norm, inverse):
    scaled = grad * gain
    return inverse * (
        scaled
        - jnp.mean(scaled, axis=-1, keepdims=True)
        - norm * jnp.mean(scaled * norm, axis=-1, keepdims=True)
    )


def gelu_pair(u):
    k = 0.7978845608028654
    t = jnp.tanh(k * (u + 0.044715 * u * u * u))
    value = 0.5 * u * (1.0 + t)
    slope = 0.5 * (1.0 + t) + 0.5 * u * (1.0 - t * t) * k * (1.0 + 3 * 0.044715 * u * u)
    return value, slope


def body(
    tokens,
    ln1_gain,
    ln1_bias,
    qkv_weight,
    qv_bias,
    proj_weight,
    proj_bias,
    ln2_gain,
    ln2_bias,
    fc_weight,
    fc_bias,
    out_weight,
    out_bias,
    piece_starts,
    seq_lengths,
    cotangent,
):
    core = lax.axis_index("c")
    line = lax.axis_index(LINE)
    length = lax.dynamic_index_in_dim(seq_lengths, lax.axis_index("x"), 0, False)
    info = jnp.stack([core.astype(jnp.int32), length, piece_starts[0, 0], piece_starts[0, 1]])

    small = jnp.stack([ln1_gain, ln1_bias, proj_bias, ln2_gain, ln2_bias, out_bias], axis=1)
    small = jnp.pad(small, ((0, 0), (0, 122)))
    pay_q = jnp.concatenate([qkv_weight.reshape(16, 1536), small], axis=1)
    own_q = spread_out(pay_q).reshape(512, 1664)
    pay_r = jnp.concatenate([proj_weight.T, fc_weight, out_weight.T], axis=1)
    own_r = spread_out(after(pay_r, own_q)).reshape(512, 4608)
    all_q = jnp.concatenate([own_q, swap(own_q, "c")], axis=0)
    w_qkv = all_q[:, :1536]
    vectors = all_q[:, 1536:1544].astype(f32).T
    gain_one, shift_one, b_proj, gain_two, shift_two, b_out = [vectors[i : i + 1] for i in range(6)]

    order = feature_order(core)
    inputs = jnp.dot(tokens[0], order, preferred_element_type=f32)
    position = (line * 2 + core) * 256 + jnp.arange(256, dtype=jnp.int32)
    valid = (position < length).astype(f32)[:, None]
    grad_final = jnp.dot(cotangent[0], order, preferred_element_type=f32) * valid
    grad_mlp = low(grad_final)

    norm_one, inv_one = norm_parts(inputs)
    normed = low(norm_one * gain_one + shift_one)
    bias = qv_bias.astype(f32)
    bias3 = jnp.concatenate([bias[0], jnp.zeros((512,), f32), bias[1]])
    project = low(contract(w_qkv, normed, 0, 1) + bias3[:, None])
    heads = project.reshape(3, 8, 64, 256).transpose(1, 0, 2, 3).reshape(8, 192, 256)
    own = exchange(heads, LINE)
    other = swap(own[:, 64:], "c")
    attended, attended_low, log_sum = attn_forward(info, own, other)
    heads_out = exchange(attended_low, LINE).reshape(512, 256)

    all_r = jnp.concatenate([own_r, swap(own_r, "c")], axis=0)
    w_proj = all_r[:, :512]
    w_fc = all_r[:, 512:2560]
    w_out = all_r[:, 2560:]

    attn_part = low(contract(heads_out, w_proj, 0, 1))
    attn_out = attn_part.astype(f32) + swap(attn_part, "tp").astype(f32) + b_proj
    middle = inputs + attn_out
    norm_two, inv_two = norm_parts(middle)
    normed_two = low(norm_two * gain_two + shift_two)
    hidden = jnp.dot(normed_two, w_fc, preferred_element_type=f32) + fc_bias.astype(f32)
    value, slope = gelu_pair(hidden)
    activated = low(value)
    grad_act = jnp.dot(grad_mlp, w_out, preferred_element_type=f32)
    grad_hidden = low(grad_act * slope)
    norm_two_part = low(contract(grad_hidden, w_fc, 1, 1))
    grad_norm_two = norm_two_part.astype(f32) + swap(norm_two_part, "tp").astype(f32)
    mlp_part = low(contract(activated, w_out, 1, 1))
    mlp_out = mlp_part.astype(f32) + swap(mlp_part, "tp").astype(f32) + b_out
    final = middle + mlp_out

    grad_middle = grad_final + norm_back(grad_norm_two, gain_two, norm_two, inv_two)
    grad_attn = low(grad_middle)
    grad_heads = low(contract(w_proj, grad_attn, 0, 1)).reshape(8, 64, 256)
    grad_mine = exchange(grad_heads, LINE)
    grad_query, grad_own, grad_other = attn_backward(
        info, own, other, grad_mine, attended, log_sum
    )

    grad_proj = contract(grad_attn, heads_out, 0, 1)
    grad_fc = contract(normed_two, grad_hidden, 0, 0)
    grad_out = contract(grad_mlp, activated, 0, 0)

    def squares(field):
        return jnp.sum(valid * field * field)

    roots = jnp.stack([squares(inputs), squares(attn_out), squares(mlp_out), squares(final)])
    columns = jnp.stack(
        [
            jnp.sum(grad_attn.astype(f32), axis=0),
            jnp.sum(grad_norm_two * norm_two, axis=0),
            jnp.sum(grad_norm_two, axis=0),
            jnp.sum(grad_mlp.astype(f32), axis=0),
        ],
        axis=1,
    )
    fc_sums = jnp.sum(grad_hidden.astype(f32), axis=0).reshape(16, 128)
    shared = jnp.concatenate([fc_sums, jnp.broadcast_to(roots[None], (16, 4))], axis=1)
    shared = jnp.broadcast_to(shared[None], (64, 16, 132)).reshape(1024, 132)
    pay_g = jnp.concatenate(
        [grad_proj, grad_fc, grad_out, shared, columns, jnp.zeros((1024, 120), f32)], axis=1
    )

    def scatter(pay):
        mine, theirs = pay[:512], low(pay[512:])
        both = low(mine + swap(theirs, "c").astype(f32))
        got = exchange(both.reshape(32, 16, -1), SPREAD)
        return jnp.sum(got.astype(f32), axis=0)

    got_g = scatter(pay_g)

    grad_kv = low(grad_own + swap(grad_other, "c").astype(f32))
    grad_back = exchange(jnp.concatenate([grad_query, grad_kv], axis=1), LINE)
    grad_project = grad_back.reshape(8, 3, 64, 256).transpose(1, 0, 2, 3).reshape(1536, 256)
    norm_one_part = low(contract(grad_project, w_qkv, 0, 1))
    grad_normed = norm_one_part.astype(f32) + swap(norm_one_part, "tp").astype(f32)
    grad_inputs = grad_middle + norm_back(grad_normed, gain_one, norm_one, inv_one)

    grad_qkv = contract(normed, grad_project, 0, 1)
    part = norm_one_part.astype(f32)
    columns = jnp.stack([jnp.sum(part * norm_one, axis=0), jnp.sum(part, axis=0)], axis=1)
    sums = jnp.sum(grad_project.astype(f32), axis=1)
    sums = jnp.concatenate([sums[:512], sums[1024:]]).reshape(16, 64)
    sums = jnp.broadcast_to(sums[None], (64, 16, 64)).reshape(1024, 64)
    got_q = scatter(
        jnp.concatenate([grad_qkv, sums, columns, jnp.zeros((1024, 62), f32)], axis=1)
    )

    ln1 = got_q[:, 1600:1602]
    ln1 = ln1 + swap(ln1, "tp")
    root_sum = got_g[0, 4736:4740]
    valid_total = jnp.sum(seq_lengths).astype(f32)
    root_squares = jnp.sqrt(root_sum / (valid_total * 1024) + ROOT_EPS)
    return (
        low(contract(low(final), order, 1, 1))[None],
        low(contract(low(grad_inputs), order, 1, 1))[None],
        ln1[:, 0],
        ln1[:, 1],
        got_q[:, :1536].reshape(16, 3, 512),
        got_q[:, 1536:1600].reshape(2, 512),
        got_g[:, :512].T,
        got_g[:, 4740],
        got_g[:, 4741],
        got_g[:, 4742],
        got_g[:, 512:2560],
        got_g[:, 4608:4736].reshape(2048),
        got_g[:, 2560:4608].T,
        got_g[:, 4743],
        root_squares,
    )


def solution(mesh):
    fine = Mesh(mesh.devices.reshape(4, 2, 4, 2, 2), ("x", "zh", "y", "c", "tp"))
    ctx = ("zh", "y", "c")
    every = ("x", "zh", "y", "c")
    in_specs = (
        P("x", ctx, None),
        P(every),
        P(every),
        P(every, None, "tp"),
        P(None, "tp"),
        P("tp", every),
        P(every),
        P(every),
        P(every),
        P(every, "tp"),
        P("tp"),
        P("tp", every),
        P(every),
        P("x", None),
        P(),
        P("x", ctx, None),
    )
    out_specs = (
        P("x", ctx, None),
        P("x", ctx, None),
        P(every),
        P(every),
        P(every, None, "tp"),
        P(None, "tp"),
        P("tp", every),
        P(every),
        P(every),
        P(every),
        P(every, "tp"),
        P("tp"),
        P("tp", every),
        P(every),
        P(),
    )
    return jax.shard_map(body, mesh=fine, in_specs=in_specs, out_specs=out_specs, check_vma=False)
```

time: 2500 us -> 486 us (0.19)
  waiting for transfers between devices: 1440 us -> 157 us
  blocking collectives: 661 us -> 92.4 us
  matrix products: 190 us -> 51.5 us
  Pallas kernels: 0 us -> 43.8 us
  local copies, waits for them, and re-layouts: 104 us -> 63.5 us
  other arithmetic: 72.3 us -> 35.1 us
  starting transfers between devices: 1.24 us -> 36.1 us
    reduce_scatter x6 -> x0, waiting for transfers between devices: 1170 us -> none  [the longest x1 343 us: body(): lax.psum_scatter(grad_out, ('fsdp', 'ctx'), scatter_dimension=1, tiled=True)]
    unnamed x2 -> x0, blocking collectives: 661 us -> none
    all_gather x6 -> x0, waiting for transfers between devices: 191 us -> none  [the longest x1 75.2 us: body(): lax.all_gather(fc_weight, ('fsdp', 'ctx'), axis=0, tiled=True)]
    dot_general x68 -> x16, matrix products: 190 us -> 51.5 us  [the longest x12 40.6 us: contract(): lax.dot_general(a, b, (((dim_a,), (dim_b,)), ((), ())), preferred_element...]
    all_to_all x0 -> x5, waiting for transfers between devices: none -> 105 us  [exchange(): return lax.all_to_all(field, axes, split_axis=0, concat_axis=0, tiled=True)]
    all_to_all x0 -> x3, blocking collectives: none -> 92.4 us  [exchange(): return lax.all_to_all(field, axes, split_axis=0, concat_axis=0, tiled=True)]
    psum x3 -> x0, waiting for transfers between devices: 83.8 us -> none  [the longest x1 43.5 us: body(): lax.psum(jnp.dot(activated, w_out, preferred_element_type=jnp.float32).as...]
    ppermute x0 -> x11, waiting for transfers between devices: none -> 52 us  [swap(): return lax.ppermute(field, axis, [(0, 1), (1, 0)])]
  transfers between devices with their start and end apart: 15 -> 16, of which waited for: 11 -> 13; matrix products, arithmetic and copies ran while one was open for 8% -> 16% of each run, Pallas kernels for 0% -> 4%
where the time goes in v1:
time: 486 us; the launch traced here: 481 us
  waiting for transfers between devices  157 us (32%)
  blocking collectives  92.4 us (19%)
  local copies, waits for them, and re-layouts  63.5 us (13%)
  matrix products  51.5 us (11%)
  Pallas kernels  43.8 us (9%)
  starting transfers between devices  36.1 us (7%)
  other arithmetic  35.1 us (7%)
    all_to_all x5, waiting for transfers between devices, exchange(): return lax.all_to_all(field, axes, split_axis=0, concat_axis=0, tiled=True)  105 us
    all_to_all x3, blocking collectives, exchange(): return lax.all_to_all(field, axes, split_axis=0, concat_axis=0, tiled=True)  92.4 us
    ppermute x11, waiting for transfers between devices, swap(): return lax.ppermute(field, axis, [(0, 1), (1, 0)])  52 us
    dot_general x12, matrix products, contract(): lax.dot_general(a, b, (((dim_a,), (dim_b,)), ((), ())), preferred_element...  40.6 us
    all_to_all x5, starting transfers between devices, exchange(): return lax.all_to_all(field, axes, split_axis=0, concat_axis=0, tiled=True)  29.2 us
    pallas_call x1, Pallas kernels, attn_backward(): pl.pallas_call(backward_kernel, out_shape=(jax.ShapeDtypeStruct((H, E, B)...  25.1 us
    concatenate x1, local copies, waits for them, and re-layouts, body(): jnp.concatenate([grad_proj, grad_fc, grad_out, shared, columns, jnp.zeros...  22 us
    pallas_call x1, Pallas kernels, attn_forward(): pl.pallas_call(forward_kernel, out_shape=(jax.ShapeDtypeStruct((H, E, B),...  18.7 us
  transfers between devices with their start and end apart: 16, of which 13 were waited for; matrix products, arithmetic and copies ran while one was open for 16% of the time, Pallas kernels for 4%

profile of v1, /device:TPU:0, one launch (start us, length us, event | category | flops | bytes accessed | tf_op | source)
XLA Modules:
  0.0 481.4 jit_solution(786312526868968977)
XLA Ops:
  7.4 10.7 %all-to-all-start = ((bf16[32,16,1664]{2,1,0:T(8,128)(2,1)}), bf16[32,16,1664]{2,1,0:T(8,128)(2,1)S(1)}, u32[]{:S(2)}, u32[]{:S(2)}) async-start(bf16[32,16,1664]{2,1,0:T(8,128)(2,1)} %broadcast_in_dim.30), calls=%async_computation | async-start | bytes 3407872 | tf_op jit(solution)/shard_map/all_to_all | solution.py:153
  18.2 24.6 %all-to-all-done = bf16[32,16,1664]{2,1,0:T(8,128)(2,1)S(1)} async-done(((bf16[32,16,1664]{2,1,0:T(8,128)(2,1)}), bf16[32,16,1664]{2,1,0:T(8,128)(2,1)S(1)}, u32[]{:S(2)}, u32[]{:S(2)}) %all-to-all-start) | async-done | bytes 1703968 | tf_op jit(solution)/shard_map/all_to_all | solution.py:153
  43.4 63.5 %all_to_all.40 = bf16[32,16,4608]{2,1,0:T(8,128)(2,1)} all-to-all(bf16[32,16,4608]{2,1,0:T(8,128)(2,1)S(1)} %broadcast_in_dim.32), channel_id=1, replica_groups=mesh['x'=4,'zh'=2,'y'=4,'c'=2,'tp'=2] {'x','zh','y'}, dimensions={0} | all-to-all | bytes 9437184 | tf_op jit(solution)/shard_map/all_to_all | solution.py:153
  108.4 8.5 %collective-permute-done = bf16[512,1664]{1,0:T(8,128)(2,1)} collective-permute-done((bf16[512,1664]{1,0:T(8,128)(2,1)S(1)}, bf16[512,1664]{1,0:T(8,128)(2,1)}, u32[]{:S(2)}, u32[]{:S(2)}) %collective-permute-start) | collective-permute-done | bytes 1703968 | tf_op jit(solution)/shard_map/ppermute | solution.py:149
  117.9 1.6 slice_reduce_fusion
  119.5 2.9 fusion.10
  122.5 17.6 %all_to_all.41.own_ref = bf16[8,192,256]{2,1,0:T(8,128)(2,1)S(1)} all-to-all(bf16[8,192,256]{2,1,0:T(8,128)(2,1)S(1)} %bitcast.115), channel_id=1, replica_groups=mesh['x'=4,'zh'=2,'y'=4,'c'=2,'tp'=2] {'zh','y'}, dimensions={0} | all-to-all | bytes 1572864 | tf_op jit(solution)/shard_map/all_to_all | solution.py:153
  141.4 2.0 pad_add_fusion.info_ref
  143.5 18.7 %attention_forward.1 = (f32[8,64,256]{2,1,0:T(8,128)S(1)}, bf16[8,64,256]{2,1,0:T(8,128)(2,1)}, f32[8,1,256]{2,1,0:T(1,128)S(1)}) custom-call(s32[4]{0:T(128)S(1)} %pad_add_fusion.info_ref, bf16[8,192,256]{2,1,0:T(8,128)(2,1)S(1)} %all_to_all.41.own_ref, bf16[8,128,256]{2,1,0:T(8,128)(2,1)S(1)} %collective-permute-done.1.other_ref), custom_call_target="tpu_custom_call" | custom-call | flops 1207959552 | bytes 3145728 | tf_op jit(solution)/shard_map/attention_forward/pallas_call | solution.py:121
  162.2 3.4 all-to-all-start.2
  166.9 8.7 %all-to-all-done.2 = bf16[8,64,256]{2,1,0:T(8,128)(2,1)S(1)} async-done(((bf16[8,64,256]{2,1,0:T(8,128)(2,1)}), bf16[8,64,256]{2,1,0:T(8,128)(2,1)S(1)}, u32[]{:S(2)}, u32[]{:S(2)}) %all-to-all-start.2) | async-done | bytes 262176 | tf_op jit(solution)/shard_map/all_to_all | solution.py:153
  179.6 1.9 fusion.24
  181.6 10.4 %collective-permute-done.3 = bf16[256,1024]{0,1:T(8,128)(2,1)} collective-permute-done((bf16[256,1024]{0,1:T(8,128)(2,1)S(1)}, bf16[256,1024]{0,1:T(8,128)(2,1)}, u32[]{:S(2)}, u32[]{:S(2)}) %collective-permute-start.3) | collective-permute-done | bytes 524320 | tf_op jit(solution)/shard_map/ppermute | solution.py:149
  193.4 3.6 convolution_add_fusion.1
  197.1 4.4 convolution_convert_fusion.3
  202.6 4.6 convert_reduce_fusion.2
  207.2 3.9 convolution_convert_fusion.2
  212.2 4.2 collective-permute-done.4
  216.4 9.4 %collective-permute-done.5 = bf16[256,1024]{0,1:T(8,128)(2,1)S(1)} collective-permute-done((bf16[256,1024]{0,1:T(8,128)(2,1)S(1)}, bf16[256,1024]{0,1:T(8,128)(2,1)S(1)}, u32[]{:S(2)}, u32[]{:S(2)}) %collective-permute-start.5) | collective-permute-done | bytes 524320 | tf_op jit(solution)/shard_map/ppermute | solution.py:149
  225.8 3.1 fusion.35
  230.6 11.3 %all_to_all.42.gout_ref = bf16[8,64,256]{2,1,0:T(8,128)(2,1)S(1)} all-to-all(bf16[8,64,256]{2,1,0:T(8,128)(2,1)S(1)} %bitcast.119), channel_id=1, replica_groups=mesh['x'=4,'zh'=2,'y'=4,'c'=2,'tp'=2] {'zh','y'}, dimensions={0} | all-to-all | bytes 524288 | tf_op jit(solution)/shard_map/all_to_all | solution.py:153
  241.9 25.1 %attention_backward.1 = (bf16[8,64,256]{2,1,0:T(8,128)(2,1)S(1)}, f32[8,128,256]{2,1,0:T(8,128)S(1)}, bf16[8,128,256]{2,1,0:T(8,128)(2,1)S(1)}) custom-call(s32[4]{0:T(128)S(1)} %pad_add_fusion.info_ref, bf16[8,192,256]{2,1,0:T(8,128)(2,1)S(1)} %all_to_all.41.own_ref, bf16[8,128,256]{2,1,0:T(8,128)(2,1)S(1)} %collective-permute-done.1.other_ref, ...), custom_call_target="tpu_custom_call" | custom-call | flops 3019898880 | bytes 5242880 | tf_op jit(solution)/shard_map/attention_backward/pallas_call | solution.py:130
  267.3 1.9 collective-permute-done.6
  270.3 3.5 all-to-all-start.5
  273.8 6.4 %fusion.75 = f32[1024,2048]{1,0:T(8,128)} fusion(f32[256,1024]{0,1:T(8,128)S(1)} %copy-done.13, f32[256,2048]{1,0:T(8,128)} %copy-done.8), kind=kOutput, calls=%fused_computation.170 | convolution fusion | flops 1078722560 | bytes 11534336 | tf_op jit(solution)/shard_map/dot_general | solution.py:165
  280.2 8.5 %all-to-all-done.5 = bf16[8,192,256]{2,1,0:T(8,128)(2,1)S(1)} async-done(((bf16[8,192,256]{2,1,0:T(8,128)(2,1)}), bf16[8,192,256]{2,1,0:T(8,128)(2,1)S(1)}, u32[]{:S(2)}, u32[]{:S(2)}) %all-to-all-start.5) | async-done | bytes 786464 | tf_op jit(solution)/shard_map/all_to_all | solution.py:153
  288.8 4.0 convolution_convert_fusion.1
  293.7 4.6 fusion.81
  302.5 3.1 fusion.72
  306.7 2.6 fusion.32
  309.3 2.7 pad_maximum_fusion.13
  313.8 22.0 %concatenate.46 = f32[1024,4864]{1,0:T(8,128)} concatenate(f32[1024,512]{1,0:T(8,128)} %fusion.72, f32[1024,2048]{1,0:T(8,128)} %fusion.81, f32[1024,2048]{1,0:T(8,128)} %fusion.75, f32[1024,132]{1,0:T(8,128)} %bitcast.112, f32[1024,1]{1,0:T(8,128)S(1)} %copy-done.18, f32[1024,1]{1,0:T(8,128)} %copy.81, f32[1024,1]{1,0:T(8,128)} %copy.82, f32[1024,1]{1,0:T(8,128)} %copy.83, ...), dimensions={1} | concatenate | bytes 39845888 | tf_op jit(solution)/shard_map/concatenate | solution.py:300
  335.8 6.6 %slice.222 = bf16[512,4864]{1,0:T(8,128)(2,1)} slice(f32[1024,4864]{1,0:T(8,128)} %concatenate.46), slice={[512:1024], [0:4864]} | slice | bytes 9961472 | tf_op jit(solution)/shard_map/slice | solution.py:305
  342.7 3.7 fusion.80
  348.6 8.4 %concatenate.44 = f32[1024,1664]{1,0:T(8,128)} concatenate(f32[1024,1536]{1,0:T(8,128)} %fusion.80, f32[1024,64]{1,0:T(8,128)} %bitcast.118, f32[1024,1]{1,0:T(8,128)S(1)} %copy.77, f32[1024,1]{1,0:T(8,128)S(1)} %copy.78, f32[1024,62]{1,0:T(8,128)} %broadcast_in_dim.36), dimensions={1} | concatenate | bytes 13631488 | tf_op jit(solution)/shard_map/concatenate | solution.py:326
  357.0 2.1 slice.223
  359.7 3.2 collective-permute-done.8
  362.9 3.4 fusion.4
  366.3 4.7 all-to-all-start.6
  371.1 8.5 %fusion = bf16[512,4864]{1,0:T(8,128)(2,1)} fusion(f32[1024,4864]{1,0:T(8,128)} %concatenate.46, bf16[512,4864]{1,0:T(8,128)(2,1)} %collective-permute-done.10), kind=kLoop, calls=%fused_computation.2 | loop fusion | flops 7471104 | bytes 19922944 | tf_op jit(solution)/shard_map/convert_element_type | solution.py:145
  379.6 16.6 %all-to-all-done.6 = bf16[32,16,1664]{2,1,0:T(8,128)(2,1)} async-done(((bf16[32,16,1664]{2,1,0:T(8,128)(2,1)}), bf16[32,16,1664]{2,1,0:T(8,128)(2,1)}, u32[]{:S(2)}, u32[]{:S(2)}) %all-to-all-start.6) | async-done | bytes 1703968 | tf_op jit(solution)/shard_map/all_to_all | solution.py:153
  396.2 6.8 %all-to-all-start.7 = ((bf16[32,16,4864]{2,1,0:T(8,128)(2,1)}), bf16[32,16,4864]{2,1,0:T(8,128)(2,1)}, u32[]{:S(2)}, u32[]{:S(2)}) async-start(bf16[32,16,4864]{2,1,0:T(8,128)(2,1)} %bitcast.104), calls=%async_computation.7 | async-start | bytes 9961472 | tf_op jit(solution)/shard_map/all_to_all | solution.py:153
  404.3 2.1 fusion.30
  406.3 3.8 fusion.29
  410.1 1.7 convert_reduce_fusion.1
  414.2 13.3 %collective-permute-done.9 = f32[16,2]{1,0:T(8,128)S(1)} collective-permute-done((f32[16,2]{1,0:T(8,128)S(1)}, f32[16,2]{1,0:T(8,128)S(1)}, u32[]{:S(2)}, u32[]{:S(2)}) %collective-permute-start.9) | collective-permute-done | bytes 160 | tf_op jit(solution)/shard_map/ppermute | solution.py:149
  428.3 46.7 %all-to-all-done.7 = bf16[32,16,4864]{2,1,0:T(8,128)(2,1)} async-done(((bf16[32,16,4864]{2,1,0:T(8,128)(2,1)}), bf16[32,16,4864]{2,1,0:T(8,128)(2,1)}, u32[]{:S(2)}, u32[]{:S(2)}) %all-to-all-start.7) | async-done | bytes 4980768 | tf_op jit(solution)/shard_map/all_to_all | solution.py:153
  475.0 3.2 convert_reduce_fusion
  (143 shorter events, 41.4 us)
Async XLA Ops:
  0.6 106.8 %copy-start = (bf16[1,256,1024]{2,1,0:T(8,128)(2,1)S(1)}, bf16[1,256,1024]{2,1,0:T(8,128)(2,1)}, u32[]{:S(2)}) copy-start(bf16[1,256,1024]{2,1,0:T(8,128)(2,1)} %param.16) | copy-start | bytes 1572868
  0.7 17.5 %copy-start.23 = (bf16[2048,16]{0,1:T(8,128)(2,1)S(1)}, bf16[2048,16]{0,1:T(8,128)(2,1)}, u32[]{:S(2)}) copy-start(bf16[2048,16]{0,1:T(8,128)(2,1)} %param.27) | copy-start | bytes 196612
  0.7 17.5 %copy-start.24 = (bf16[16,2048]{1,0:T(8,128)(2,1)S(1)}, bf16[16,2048]{1,0:T(8,128)(2,1)}, u32[]{:S(2)}) copy-start(bf16[16,2048]{1,0:T(8,128)(2,1)} %param.25) | copy-start | bytes 196612
  0.7 17.5 %copy-start.25 = (bf16[512,16]{0,1:T(8,128)(2,1)S(1)}, bf16[512,16]{0,1:T(8,128)(2,1)}, u32[]{:S(2)}) copy-start(bf16[512,16]{0,1:T(8,128)(2,1)} %param.21) | copy-start | bytes 49156
  7.4 35.4 %all-to-all-start = ((bf16[32,16,1664]{2,1,0:T(8,128)(2,1)}), bf16[32,16,1664]{2,1,0:T(8,128)(2,1)S(1)}, u32[]{:S(2)}, u32[]{:S(2)}) async-start(bf16[32,16,1664]{2,1,0:T(8,128)(2,1)} %broadcast_in_dim.30), calls=%async_computation | async-start | bytes 3407872 | tf_op jit(solution)/shard_map/all_to_all | solution.py:153
  42.8 76.7 %copy-start.9 = (bf16[32,16,1664]{2,1,0:T(8,128)(2,1)}, bf16[32,16,1664]{2,1,0:T(8,128)(2,1)S(1)}, u32[]{:S(2)}) copy-start(bf16[32,16,1664]{2,1,0:T(8,128)(2,1)S(1)} %all-to-all-done) | copy-start | bytes 5111812
  43.4 64.0 %copy-start.26 = (bf16[2,512]{1,0:T(2,128)(2,1)S(1)}, bf16[2,512]{1,0:T(2,128)(2,1)}, u32[]{:S(2)}) copy-start(bf16[2,512]{1,0:T(2,128)(2,1)} %param.20) | copy-start | bytes 6148
  106.9 58.7 %collective-permute-start.2 = (bf16[512,4608]{1,0:T(8,128)(2,1)}, bf16[512,4608]{1,0:T(8,128)(2,1)}, u32[]{:S(2)}, u32[]{:S(2)}) collective-permute-start(bf16[512,4608]{1,0:T(8,128)(2,1)} %bitcast.21), channel_id=1, source_target_pairs={{0,2},{2,0},{1,3},{3,1},{4,6},{6,4},{5,7},{7,5},{8,10},{10,8},{9,1... | collective-permute-start | bytes 14155784 | tf_op jit(solution)/shard_map/ppermute | solution.py:149
  106.9 10.1 %collective-permute-start = (bf16[512,1664]{1,0:T(8,128)(2,1)S(1)}, bf16[512,1664]{1,0:T(8,128)(2,1)}, u32[]{:S(2)}, u32[]{:S(2)}) collective-permute-start(bf16[512,1664]{1,0:T(8,128)(2,1)S(1)} %bitcast.107), channel_id=1, source_target_pairs={{0,2},{2,0},{1,3},{3,1},{4,6},{6,4},{5,7},{7,5},{8,10},{10,8},{9,1... | collective-permute-start | bytes 5111816 | tf_op jit(solution)/shard_map/ppermute | solution.py:149
  108.2 11.3 %copy-start.2 = (f32[1024,256]{1,0:T(8,128)}, f32[1024,256]{1,0:T(8,128)S(1)}, u32[]{:S(2)}) copy-start(f32[1024,256]{1,0:T(8,128)S(1)} %get-tuple-element.100) | copy-start | bytes 3145732
  122.4 17.9 %copy-start.29 = (s32[4]{0:T(128)S(1)}, s32[4]{0:T(128)}, u32[]{:S(2)}) copy-start(s32[4]{0:T(128)} %param.30) | copy-start | bytes 52
  122.4 18.4 %copy-start.28 = (s32[1,2]{1,0:T(1,128)S(1)}, s32[1,2]{1,0:T(1,128)}, u32[]{:S(2)}) copy-start(s32[1,2]{1,0:T(1,128)} %param.29) | copy-start | bytes 28
  140.2 3.3 collective-permute-start.1
  162.2 13.5 %all-to-all-start.2 = ((bf16[8,64,256]{2,1,0:T(8,128)(2,1)}), bf16[8,64,256]{2,1,0:T(8,128)(2,1)S(1)}, u32[]{:S(2)}, u32[]{:S(2)}) async-start(bf16[8,64,256]{2,1,0:T(8,128)(2,1)} %get-tuple-element.22), calls=%async_computation.2 | async-start | bytes 524288 | tf_op jit(solution)/shard_map/all_to_all | solution.py:153
  165.6 13.4 %copy-start.27 = (bf16[2048]{0:T(1024)(128)(2,1)S(1)}, bf16[2048]{0:T(1024)(128)(2,1)}, u32[]{:S(2)}) copy-start(bf16[2048]{0:T(1024)(128)(2,1)} %param.26) | copy-start | bytes 12292
  166.9 14.7 %copy-start.5 = (bf16[1024,512]{1,0:T(8,128)(2,1)}, bf16[1024,512]{1,0:T(8,128)(2,1)S(1)}, u32[]{:S(2)}) copy-start(bf16[1024,512]{1,0:T(8,128)(2,1)S(1)} %pad_maximum_fusion.2) | copy-start | bytes 3145732
  175.6 0.7 copy-start.16
  177.7 14.2 %collective-permute-start.3 = (bf16[256,1024]{0,1:T(8,128)(2,1)S(1)}, bf16[256,1024]{0,1:T(8,128)(2,1)}, u32[]{:S(2)}, u32[]{:S(2)}) collective-permute-start(bf16[256,1024]{0,1:T(8,128)(2,1)S(1)} %convolution_convert_fusion), channel_id=1, source_target_pairs={{0,1},{1,0},{2,3},{3,2},{4,5},{5,4},{6,7},{7,6},{8,9},{9,8},{10,11... | collective-permute-start | bytes 1572872 | tf_op jit(solution)/shard_map/ppermute | solution.py:149
  179.6 12.3 %copy-start.3 = (f32[1024,256]{1,0:T(8,128)S(1)}, f32[1024,256]{1,0:T(8,128)}, u32[]{:S(2)}) copy-start(f32[1024,256]{1,0:T(8,128)} %copy-done.2) | copy-start | bytes 3145732
  181.5 47.3 %copy-start.12 = (f32[256,1024]{0,1:T(8,128)}, f32[256,1024]{0,1:T(8,128)S(1)}, u32[]{:S(2)}) copy-start(f32[256,1024]{0,1:T(8,128)S(1)} %fusion.24) | copy-start | bytes 3145732
  197.1 5.5 %copy-start.8 = (f32[256,2048]{1,0:T(8,128)}, f32[256,2048]{1,0:T(8,128)S(1)}, u32[]{:S(2)}) copy-start(f32[256,2048]{1,0:T(8,128)S(1)} %convolution_add_fusion.1) | copy-start | bytes 6291460
  201.5 24.3 %copy-start.19 = (bf16[256,1024]{0,1:T(8,128)(2,1)}, bf16[256,1024]{0,1:T(8,128)(2,1)S(1)}, u32[]{:S(2)}) copy-start(bf16[256,1024]{0,1:T(8,128)(2,1)S(1)} %convolution_convert_fusion.3) | copy-start | bytes 1572868
  201.5 14.9 %collective-permute-start.4 = (bf16[256,1024]{0,1:T(8,128)(2,1)S(1)}, bf16[256,1024]{0,1:T(8,128)(2,1)S(1)}, u32[]{:S(2)}, u32[]{:S(2)}) collective-permute-start(bf16[256,1024]{0,1:T(8,128)(2,1)S(1)} %convolution_convert_fusion.3), channel_id=1, source_target_pairs={{0,1},{1,0},{2,3},{3,2},{4,5},{5,4},{6,7},{7,6},{8,9},{9,8},{10,11... | collective-permute-start | bytes 1572872 | tf_op jit(solution)/shard_map/ppermute | solution.py:149
  207.2 3.9 copy-start.10
  211.1 14.7 %collective-permute-start.5 = (bf16[256,1024]{0,1:T(8,128)(2,1)S(1)}, bf16[256,1024]{0,1:T(8,128)(2,1)S(1)}, u32[]{:S(2)}, u32[]{:S(2)}) collective-permute-start(bf16[256,1024]{0,1:T(8,128)(2,1)S(1)} %convolution_convert_fusion.2), channel_id=1, source_target_pairs={{0,1},{1,0},{2,3},{3,2},{4,5},{5,4},{6,7},{7,6},{8,9},{9,8},{10,11... | collective-permute-start | bytes 1572872 | tf_op jit(solution)/shard_map/ppermute | solution.py:149
  216.4 13.2 %copy-start.21 = (bf16[256,1024]{0,1:T(8,128)(2,1)}, bf16[256,1024]{0,1:T(8,128)(2,1)S(1)}, u32[]{:S(2)}) copy-start(bf16[256,1024]{0,1:T(8,128)(2,1)S(1)} %collective-permute-done.4) | copy-start | bytes 1572868
  228.9 1.2 copy-start.6
  229.6 12.3 %copy-start.7 = (f32[256,1024]{0,1:T(8,128)}, f32[256,1024]{0,1:T(8,128)S(1)}, u32[]{:S(2)}) copy-start(f32[256,1024]{0,1:T(8,128)S(1)} %get-tuple-element.87) | copy-start | bytes 3145732
  267.0 6.8 %copy-start.13 = (f32[256,1024]{0,1:T(8,128)S(1)}, f32[256,1024]{0,1:T(8,128)}, u32[]{:S(2)}) copy-start(f32[256,1024]{0,1:T(8,128)} %copy-done.12) | copy-start | bytes 3145732
  267.0 2.2 collective-permute-start.6
  270.3 18.5 %all-to-all-start.5 = ((bf16[8,192,256]{2,1,0:T(8,128)(2,1)}), bf16[8,192,256]{2,1,0:T(8,128)(2,1)S(1)}, u32[]{:S(2)}, u32[]{:S(2)}) async-start(bf16[8,192,256]{2,1,0:T(8,128)(2,1)} %pad_maximum_fusion.3), calls=%async_computation.5 | async-start | bytes 1572864 | tf_op jit(solution)/shard_map/all_to_all | solution.py:153
  288.8 4.0 copy-start.14
  288.8 4.9 %copy-start.11 = (bf16[256,2048]{1,0:T(8,128)(2,1)S(1)}, bf16[256,2048]{1,0:T(8,128)(2,1)}, u32[]{:S(2)}) copy-start(bf16[256,2048]{1,0:T(8,128)(2,1)} %copy-done.10) | copy-start | bytes 3145732
  292.8 9.7 %copy-start.17 = (bf16[8,64,256]{2,1,0:T(8,128)(2,1)S(1)}, bf16[8,64,256]{2,1,0:T(8,128)(2,1)}, u32[]{:S(2)}) copy-start(bf16[8,64,256]{2,1,0:T(8,128)(2,1)} %copy-done.16) | copy-start | bytes 786436
  292.8 13.9 %collective-permute-start.7 = (bf16[256,1024]{0,1:T(8,128)(2,1)}, bf16[256,1024]{0,1:T(8,128)(2,1)}, u32[]{:S(2)}, u32[]{:S(2)}) collective-permute-start(bf16[256,1024]{0,1:T(8,128)(2,1)} %convolution_convert_fusion.1), channel_id=1, source_target_pairs={{0,1},{1,0},{2,3},{3,2},{4,5},{5,4},{6,7},{7,6},{8,9},{9,8},{10,11... | collective-permute-start | bytes 1572872 | tf_op jit(solution)/shard_map/ppermute | solution.py:149
  298.3 8.3 %copy-start.4 = (f32[1024,256]{1,0:T(8,128)S(1)}, f32[1024,256]{1,0:T(8,128)}, u32[]{:S(2)}) copy-start(f32[1024,256]{1,0:T(8,128)} %copy-done.2) | copy-start | bytes 3145732
  305.6 8.3 %copy-start.18 = (f32[1024,1]{1,0:T(8,128)S(1)}, f32[1024,1]{1,0:T(8,128)}, u32[]{:S(2)}) copy-start(f32[1024,1]{1,0:T(8,128)} %copy.80) | copy-start | bytes 12292
  335.8 6.9 %copy-start.15 = (bf16[8,3,64,256]{3,2,0,1:T(8,128)(2,1)S(1)}, bf16[8,3,64,256]{3,2,0,1:T(8,128)(2,1)}, u32[]{:S(2)}) copy-start(bf16[8,3,64,256]{3,2,0,1:T(8,128)(2,1)} %copy-done.14) | copy-start | bytes 2359300
  342.4 28.6 %collective-permute-start.10 = (bf16[512,4864]{1,0:T(8,128)(2,1)}, bf16[512,4864]{1,0:T(8,128)(2,1)}, u32[]{:S(2)}, u32[]{:S(2)}) collective-permute-start(bf16[512,4864]{1,0:T(8,128)(2,1)} %slice.222), channel_id=1, source_target_pairs={{0,2},{2,0},{1,3},{3,1},{4,6},{6,4},{5,7},{7,5},{8,10},{10,8},{9,1... | collective-permute-start | bytes 14942216 | tf_op jit(solution)/shard_map/ppermute | solution.py:149
  359.1 3.8 collective-permute-start.8
  366.3 29.8 %all-to-all-start.6 = ((bf16[32,16,1664]{2,1,0:T(8,128)(2,1)}), bf16[32,16,1664]{2,1,0:T(8,128)(2,1)}, u32[]{:S(2)}, u32[]{:S(2)}) async-start(bf16[32,16,1664]{2,1,0:T(8,128)(2,1)} %bitcast.111), calls=%async_computation.6 | async-start | bytes 3407872 | tf_op jit(solution)/shard_map/all_to_all | solution.py:153
  396.2 8.1 %copy-start.20 = (bf16[256,1024]{0,1:T(8,128)(2,1)S(1)}, bf16[256,1024]{0,1:T(8,128)(2,1)}, u32[]{:S(2)}) copy-start(bf16[256,1024]{0,1:T(8,128)(2,1)} %copy-done.19) | copy-start | bytes 1572868
  396.2 8.1 %copy-start.22 = (bf16[256,1024]{0,1:T(8,128)(2,1)S(1)}, bf16[256,1024]{0,1:T(8,128)(2,1)}, u32[]{:S(2)}) copy-start(bf16[256,1024]{0,1:T(8,128)(2,1)} %copy-done.21) | copy-start | bytes 1572868
  396.2 78.8 %all-to-all-start.7 = ((bf16[32,16,4864]{2,1,0:T(8,128)(2,1)}), bf16[32,16,4864]{2,1,0:T(8,128)(2,1)}, u32[]{:S(2)}, u32[]{:S(2)}) async-start(bf16[32,16,4864]{2,1,0:T(8,128)(2,1)} %bitcast.104), calls=%async_computation.7 | async-start | bytes 9961472 | tf_op jit(solution)/shard_map/all_to_all | solution.py:153
  411.9 69.6 %copy-start.1 = (bf16[1,256,1024]{2,1,0:T(8,128)(2,1)S(1)}, bf16[1,256,1024]{2,1,0:T(8,128)(2,1)}, u32[]{:S(2)}) copy-start(bf16[1,256,1024]{2,1,0:T(8,128)(2,1)} %param.16) | copy-start | bytes 1572868
  411.9 15.7 %collective-permute-start.9 = (f32[16,2]{1,0:T(8,128)S(1)}, f32[16,2]{1,0:T(8,128)S(1)}, u32[]{:S(2)}, u32[]{:S(2)}) collective-permute-start(f32[16,2]{1,0:T(8,128)S(1)} %slice.163), channel_id=1, source_target_pairs={{0,1},{1,0},{2,3},{3,2},{4,5},{5,4},{6,7},{7,6},{8,9},{9,8},{10,11... | collective-permute-start | bytes 392 | tf_op jit(solution)/shard_map/ppermute | solution.py:149

commit v2 on v1

v2 whole, which is shorter than its diff:
```python
from functools import partial

import jax
import jax.numpy as jnp
from jax import lax
from jax.experimental import pallas as pl
from jax.experimental.pallas import tpu as pltpu
from jax.sharding import Mesh
from jax.sharding import PartitionSpec as P

f32 = jnp.float32
bf16 = jnp.bfloat16
NORM_EPS = 1e-05
ROOT_EPS = 1e-06
B=256; E=64; NB=16; MASKED=-1e30; PIECE=256

class Facts:
    def __init__(self, lengths_ref, starts_ref):
        self.core = lax.axis_index("c")
        self.items = (self.core, lengths_ref[lax.axis_index("x")], starts_ref[0, 0], starts_ref[0, 1])

    def __getitem__(self, at):
        return self.items[at]


def piece_of(pos, info_ref):
    n0=(pos>=info_ref[2])&(pos<info_ref[2]+PIECE)
    n1=(pos>=info_ref[3])&(pos<info_ref[3]+PIECE)
    return jnp.where(n0,1,0)+jnp.where(n1,2,0)

def allowed_block(key_block, query_block, info_ref):
    kpos=key_block*B+lax.broadcasted_iota(jnp.int32,(B,1),0)
    qpos=query_block*B+lax.broadcasted_iota(jnp.int32,(1,B),1)
    kp=piece_of(kpos,info_ref); qp=piece_of(qpos,info_ref)
    qp=jnp.where(qp==0,-1,qp)
    kp=jnp.where(kpos<info_ref[1],kp,-2)
    kpos=jnp.where(kpos<info_ref[1],kpos,1<<20)
    return (kpos<=qpos)|(kp==qp)

def extra_blocks(p, info_ref):
    edge=(2*p+2)*B
    crosses=((info_ref[2]<edge)&(edge<info_ref[2]+PIECE))|((info_ref[3]<edge)&(edge<info_ref[3]+PIECE))
    return jnp.where((info_ref[0]==1)&(p<NB//2-1)&crosses,1,0)

def dot(a,b): return jnp.dot(a,b,preferred_element_type=f32)

def forward_kernel(lengths_ref, starts_ref, own_ref, other_ref, out_ref, low_ref, lse_ref, key_ref, value_ref):
    info_ref=Facts(lengths_ref,starts_ref)
    core=info_ref[0]
    def stage(p,_):
        key_ref[2*p+core]=own_ref[p,E:2*E,:].T
        value_ref[2*p+core]=own_ref[p,2*E:,:]
        key_ref[2*p+1-core]=other_ref[p,:E,:].T
        value_ref[2*p+1-core]=other_ref[p,E:,:]
        return 0
    lax.fori_loop(0,NB//2,stage,0)
    def one(p,_):
        query=own_ref[p,:E,:]*jnp.asarray(0.125,bf16)
        qb=2*p+core
        def step(blocks,masked,carry):
            top,total,acc=carry
            scores=[dot(key_ref[j],query) for j in blocks]
            if masked: scores=[jnp.where(allowed_block(j,qb,info_ref),s,MASKED) for j,s in zip(blocks,scores)]
            new=top
            for s in scores: new=jnp.maximum(new,jnp.max(s,axis=0,keepdims=True))
            scale=jnp.exp(top-new)
            total=total*scale; acc=acc*scale
            for j,s in zip(blocks,scores):
                e=jnp.exp(s-new)
                total=total+jnp.sum(e,axis=0,keepdims=True)
                acc=acc+dot(value_ref[j],e.astype(bf16))
            return new,total,acc
        carry=(jnp.full((1,B),MASKED,f32),jnp.zeros((1,B),f32),jnp.zeros((E,B),f32))
        carry=step((2*p,2*p+1),True,carry)
        carry=lax.fori_loop(0,p,lambda i,c: step((2*i,2*i+1),False,c),carry)
        carry=lax.fori_loop(0,extra_blocks(p,info_ref),lambda i,c: step((2*p+2,),True,c),carry)
        top,total,acc=carry
        o=acc/total
        out_ref[p]=o
        low_ref[p]=o.astype(bf16)
        lse_ref[p]=top+jnp.log(total)
        return 0
    lax.fori_loop(0,NB//2,one,0)

def backward_kernel(lengths_ref, starts_ref, own_ref, other_ref, gout_ref, out_ref, lse_ref, gq_ref, gown_ref, gother_ref,
                    key_ref, keyt_ref, value_ref, gk_ref, gv_ref):
    info_ref=Facts(lengths_ref,starts_ref)
    core=info_ref[0]
    def stage(p,_):
        a=own_ref[p,E:2*E,:]; b=other_ref[p,:E,:]
        keyt_ref[2*p+core]=a; keyt_ref[2*p+1-core]=b
        key_ref[2*p+core]=a.T; key_ref[2*p+1-core]=b.T
        value_ref[2*p+core]=own_ref[p,2*E:,:].T
        value_ref[2*p+1-core]=other_ref[p,E:,:].T
        return 0
    lax.fori_loop(0,NB//2,stage,0)
    gk_ref[...]=jnp.zeros_like(gk_ref); gv_ref[...]=jnp.zeros_like(gv_ref)
    def one(p,_):
        query=own_ref[p,:E,:]*jnp.asarray(0.125,bf16)
        rows=query.T
        gout=gout_ref[p]; gout_rows=gout.T
        lse=lse_ref[p]
        delta=jnp.sum(gout.astype(f32)*out_ref[p],axis=0,keepdims=True)
        qb=2*p+core
        def step(blocks,masked,acc):
            for j in blocks:
                s=dot(key_ref[j],query)
                if masked: s=jnp.where(allowed_block(j,qb,info_ref),s,MASKED)
                e=jnp.exp(s-lse)
                gp=dot(value_ref[j],gout)
                gs=(e*(gp-delta)).astype(bf16)
                gv_ref[j]+=dot(e.astype(bf16),gout_rows)
                gk_ref[j]+=dot(gs,rows)
                acc=acc+dot(keyt_ref[j],gs)
            return acc
        acc=step((2*p,2*p+1),True,jnp.zeros((E,B),f32))
        acc=lax.fori_loop(0,p,lambda i,c: step((2*i,2*i+1),False,c),acc)
        acc=lax.fori_loop(0,extra_blocks(p,info_ref),lambda i,c: step((2*p+2,),True,c),acc)
        gq_ref[p]=(acc*0.125).astype(bf16)
        return 0
    lax.fori_loop(0,NB//2,one,0)
    def finish(p,_):
        gown_ref[p,:E,:]=gk_ref[2*p+core].T
        gown_ref[p,E:,:]=gv_ref[2*p+core].T
        gother_ref[p,:E,:]=gk_ref[2*p+1-core].T.astype(bf16)
        gother_ref[p,E:,:]=gv_ref[2*p+1-core].T.astype(bf16)
        return 0
    lax.fori_loop(0,NB//2,finish,0)

VM=pl.BlockSpec(memory_space=pltpu.VMEM); SM=pl.BlockSpec(memory_space=pltpu.SMEM)
LIMIT=40*1024*1024
def attn_forward(lengths,starts,own,other):
    H=NB//2
    return pl.pallas_call(forward_kernel,
        out_shape=(jax.ShapeDtypeStruct((H,E,B),f32),jax.ShapeDtypeStruct((H,E,B),bf16),jax.ShapeDtypeStruct((H,1,B),f32)),
        in_specs=[SM,SM,VM,VM],out_specs=(VM,VM,VM),
        scratch_shapes=[pltpu.VMEM((NB,B,E),bf16),pltpu.VMEM((NB,E,B),bf16)],
        compiler_params=pltpu.CompilerParams(vmem_limit_bytes=LIMIT),
        cost_estimate=takes(4),
        name="attention_forward")(lengths,starts,own,other)
def attn_backward(lengths,starts,own,other,gout,out,lse):
    H=NB//2
    return pl.pallas_call(backward_kernel,
        out_shape=(jax.ShapeDtypeStruct((H,E,B),bf16),jax.ShapeDtypeStruct((H,2*E,B),f32),jax.ShapeDtypeStruct((H,2*E,B),bf16)),
        in_specs=[SM,SM]+[VM]*5,out_specs=(VM,VM,VM),
        scratch_shapes=[pltpu.VMEM((NB,B,E),bf16),pltpu.VMEM((NB,E,B),bf16),pltpu.VMEM((NB,B,E),bf16),pltpu.VMEM((NB,B,E),f32),pltpu.VMEM((NB,B,E),f32)],
        compiler_params=pltpu.CompilerParams(vmem_limit_bytes=LIMIT),
        cost_estimate=takes(26),
        name="attention_backward")(lengths,starts,own,other,gout,out,lse)


SPREAD = ("x", "y", "zh")
LINE = ("zh", "y")
VM = pl.BlockSpec(memory_space=pltpu.VMEM)
SM = pl.BlockSpec(memory_space=pltpu.SMEM)
ANY = pl.BlockSpec(memory_space=pl.ANY)
ROOMY = pltpu.CompilerParams(vmem_limit_bytes=40 * 1024 * 1024)
WHOLE = pltpu.CompilerParams(vmem_limit_bytes=58 * 1024 * 1024)


def takes(microseconds):
    return pl.CostEstimate(
        flops=int(microseconds * 1.15e9), bytes_accessed=1 << 20, transcendentals=0
    )


def low(field):
    return field.astype(bf16)


def swap(field, axis):
    return lax.ppermute(field, axis, [(0, 1), (1, 0)])


def exchange(field, axes):
    return lax.all_to_all(field, axes, split_axis=0, concat_axis=0, tiled=True)


def after(field, *others):
    return lax.optimization_barrier((field, *others))[0]


def contract(a, b, dim_a, dim_b):
    return lax.dot_general(a, b, (((dim_a,), (dim_b,)), ((), ())), preferred_element_type=f32)


def shape(*dims, kind=bf16):
    return jax.ShapeDtypeStruct(dims, kind)


def far(field):
    return pltpu.with_memory_space_constraint(field, pltpu.HBM)


def block_of(array):
    dims = len(array.shape)
    return pl.BlockSpec(array.shape, lambda *_: (0,) * dims)


def call(kernel, name, outs, *args, scalars=0, cost=1, scratch=()):
    return pl.pallas_call(
        kernel,
        grid=(1,),
        out_shape=outs,
        in_specs=[SM] * scalars + [block_of(a) for a in args[scalars:]],
        out_specs=jax.tree.map(block_of, outs),
        scratch_shapes=list(scratch),
        compiler_params=ROOMY,
        cost_estimate=takes(cost),
        name=name,
    )(*args)


def feature_order(order_ref):
    place = lax.broadcasted_iota(jnp.int32, (1, 1024), 1)
    group = (place & 511) >> 4
    canon = ((group >> 3) << 3) + ((group & 1) << 2) + ((group >> 1) & 3)
    feature = ((canon * 2 + (lax.axis_index("c") ^ (place >> 9))) << 4) + (place & 15)
    for at in range(0, 1024, 256):
        rows = at + lax.broadcasted_iota(jnp.int32, (256, 1024), 0)
        order_ref[at : at + 256, :] = jnp.where(rows == feature, 1.0, 0.0).astype(bf16)


def valid_rows(lengths_ref):
    ctx = (lax.axis_index("zh") * 4 + lax.axis_index("y")) * 2 + lax.axis_index("c")
    position = ctx * 256 + lax.broadcasted_iota(jnp.int32, (256, 1), 0)
    return jnp.where(position < lengths_ref[lax.axis_index("x")], 1.0, 0.0)


def norm_parts(values):
    center = values - jnp.mean(values, axis=-1, keepdims=True)
    inverse = lax.rsqrt(jnp.mean(center * center, axis=-1, keepdims=True) + NORM_EPS)
    return center * inverse, inverse


def norm_back(grad, gain, norm, inverse):
    scaled = grad * gain
    return inverse * (
        scaled
        - jnp.mean(scaled, axis=-1, keepdims=True)
        - norm * jnp.mean(scaled * norm, axis=-1, keepdims=True)
    )


def gelu_pair(u):
    k = 0.7978845608028654
    square = u * u
    t = jnp.tanh(u * (k + (k * 0.044715) * square))
    half = 0.5 + 0.5 * t
    value = u * half
    slope = half + (0.5 * u) * (1.0 - t * t) * (k + (3 * 0.044715 * k) * square)
    return value, slope


def prepare_kernel(proj_ref, qkv_ref, a_ref, b_ref, c_ref, d_ref, e_ref, g_ref, out_ref):
    rows = [r[...].astype(f32) for r in (a_ref, b_ref, c_ref, d_ref, e_ref, g_ref)]
    small = jnp.concatenate(rows + [jnp.zeros((2, 16), f32)], axis=0).T
    small = low(jnp.concatenate([small, jnp.zeros((16, 120), f32)], axis=1))

    def one(k, _):
        out_ref[k, :, :512] = proj_ref[...]
        for c in range(3):
            out_ref[k, :, 512 * (c + 1) : 512 * (c + 2)] = qkv_ref[:, c, :]
        out_ref[k, :, 2048:] = small
        return 0

    lax.fori_loop(0, 32, one, 0)


def prepare_rest_kernel(fc_ref, out_ref, rest_ref):
    rest_ref[:, :2048] = fc_ref[...]
    rest_ref[:, 2048:] = out_ref[...]


def inputs_kernel(lengths_ref, tokens_ref, cotangent_ref, inputs_ref, grad_ref, order_ref):
    feature_order(order_ref)
    inputs_ref[...] = low(dot(tokens_ref[...], order_ref[...]))
    grad = dot(cotangent_ref[...], order_ref[...]) * valid_rows(lengths_ref)
    grad_ref[...] = low(grad)


def qkv_kernel(inputs_ref, own_ref, other_ref, bias_ref, heads_ref, normed_ref, vectors_ref):
    for half, ref in ((0, own_ref), (1, other_ref)):
        vectors_ref[:, 512 * half : 512 * (half + 1)] = ref[:, 2048:].astype(f32).T[:8]
    norm, _ = norm_parts(inputs_ref[...].astype(f32))
    normed = low(norm * vectors_ref[0:1, :] + vectors_ref[1:2, :])
    normed_ref[...] = normed
    for c in range(3):
        cols = slice(512 * (c + 1), 512 * (c + 2))
        field = dot(normed[:, :512], own_ref[:, cols]) + dot(normed[:, 512:], other_ref[:, cols])
        if c != 1:
            field = field + bias_ref[c // 2 : c // 2 + 1, :].astype(f32)
        field = low(field).T
        for h in range(8):
            heads_ref[h, 64 * c : 64 * (c + 1), :] = field[64 * h : 64 * (h + 1)]


def proj_kernel(heads_ref, own_ref, other_ref, part_ref):
    rows = heads_ref[...].T
    part_ref[:, :512] = low(contract(rows, own_ref[...], 1, 1))
    part_ref[:, 512:] = low(contract(rows, other_ref[...], 1, 1))


def project_out(heads_out, own, other):
    block = pl.BlockSpec((512, 512), lambda i: (0, 0))
    return pl.pallas_call(
        proj_kernel,
        grid=(1,),
        out_shape=shape(256, 1024),
        in_specs=[pl.BlockSpec((512, 256), lambda i: (0, 0)), block, block],
        out_specs=pl.BlockSpec((256, 1024), lambda i: (0, 0)),
        compiler_params=ROOMY,
        cost_estimate=takes(2),
        name="proj",
    )(heads_out, own, other)


def grad_act_kernel(gm_ref, own_ref, out_ref):
    out_ref[...] = dot(gm_ref[...], own_ref[...])


def grad_activated(grad_mlp, own_r):
    return pl.pallas_call(
        grad_act_kernel,
        grid=(4,),
        out_shape=shape(256, 2048, kind=f32),
        in_specs=[
            pl.BlockSpec((256, 512), lambda i: (0, 0)),
            pl.BlockSpec((512, 512), lambda i: (0, 4 + i)),
        ],
        out_specs=pl.BlockSpec((256, 512), lambda i: (0, i)),
        compiler_params=ROOMY,
        cost_estimate=takes(2),
        name="grad_act",
    )(grad_mlp, far(own_r))


def feed_kernel(
    inputs_ref,
    mine_ref,
    swapped_ref,
    vectors_ref,
    gact_ref,
    gm_ref,
    bias_ref,
    own_ref,
    other_ref,
    out_ref,
    middle_ref,
    n_ref,
    act_ref,
    gh_ref,
    part_ref,
    total_ref,
):
    i = pl.program_id(0)

    @pl.when(i == 0)
    def _():
        attn_out = mine_ref[...].astype(f32) + swapped_ref[...].astype(f32) + vectors_ref[2:3, :]
        middle = inputs_ref[...].astype(f32) + attn_out
        middle_ref[...] = middle
        norm, _ = norm_parts(middle)
        n_ref[...] = low(norm * vectors_ref[3:4, :] + vectors_ref[4:5, :])
        total_ref[...] = jnp.zeros_like(total_ref)

    halves = (slice(0, 256), slice(256, 512))
    hidden = [
        dot(n_ref[:, :512], own_ref[:, cols])
        + dot(n_ref[:, 512:], other_ref[:, cols])
        + bias_ref[:, cols].astype(f32)
        for cols in halves
    ]
    for cols, field in zip(halves, hidden):
        value, slope = gelu_pair(field)
        act_ref[:, cols] = low(value)
        grad = gact_ref[:, cols] + dot(gm_ref[...], out_ref[:, cols])
        gh_ref[:, cols] = low(grad * slope)
    total_ref[:, :512] += contract(gh_ref[...], own_ref[...], 1, 1)
    total_ref[:, 512:] += contract(gh_ref[...], other_ref[...], 1, 1)

    @pl.when(i == 3)
    def _():
        part_ref[...] = low(total_ref[...])


def feed_forward(inputs, mine, swapped, vectors, grad_act, grad_mlp, fc_bias, own_r, other_r):
    def whole(*dims):
        return pl.BlockSpec(dims, lambda i: (0, 0))

    def tile(rows, first):
        return pl.BlockSpec((rows, 512), lambda i: (0, first + i))

    wide = whole(256, 1024)
    return pl.pallas_call(
        feed_kernel,
        grid=(4,),
        out_shape=(
            shape(256, 1024, kind=f32),
            shape(256, 1024),
            shape(256, 2048),
            shape(256, 2048),
            shape(256, 1024),
        ),
        in_specs=[
            wide,
            wide,
            wide,
            whole(8, 1024),
            tile(256, 0),
            pl.BlockSpec((256, 512), lambda i: (0, 1)),
            tile(1, 0),
            tile(512, 0),
            tile(512, 0),
            tile(512, 4),
        ],
        out_specs=(wide, wide, tile(256, 0), tile(256, 0), wide),
        scratch_shapes=[pltpu.VMEM((256, 1024), f32)],
        compiler_params=ROOMY,
        cost_estimate=takes(8),
        name="feed_forward",
    )(
        inputs,
        mine,
        swapped,
        vectors,
        grad_act,
        grad_mlp,
        fc_bias,
        far(own_r),
        far(other_r),
        far(other_r),
    )


def wide_kernel(
    n_ref, gh_ref, gm_ref, act_ref, own_ref, other_ref, out_ref, part_ref, left_ref, total_ref
):
    i = pl.program_id(0)
    core = lax.axis_index("c")

    @pl.when(i == 0)
    def _():
        left_ref[0] = n_ref[...].T
        left_ref[1] = gm_ref[...].T
        total_ref[...] = jnp.zeros_like(total_ref)

    def put(left, right):
        for half in (0, 1):
            rows = pl.ds(pl.multiple_of((core ^ half) * 512, 512), 512)
            out_ref[rows, :] = low(dot(left[512 * half : 512 * (half + 1)], right))

    @pl.when(i < 4)
    def _():
        put(left_ref[0], gh_ref[...])

    @pl.when(i >= 4)
    def _():
        put(left_ref[1], act_ref[...])
        total_ref[:, :512] += contract(act_ref[...], own_ref[...], 1, 1)
        total_ref[:, 512:] += contract(act_ref[...], other_ref[...], 1, 1)

    @pl.when(i == 7)
    def _():
        part_ref[...] = low(total_ref[...])


def wide_grads(normed_two, grad_hidden, grad_mlp, activated, own_r, other_r):
    whole = pl.BlockSpec((256, 1024), lambda i: (0, 0))
    weights = pl.BlockSpec((512, 512), lambda i: (0, 4 + jnp.maximum(i - 4, 0)))
    return pl.pallas_call(
        wide_kernel,
        grid=(8,),
        out_shape=(shape(1024, 4096), shape(256, 1024)),
        in_specs=[
            whole,
            pl.BlockSpec((256, 512), lambda i: (0, jnp.minimum(i, 3))),
            whole,
            pl.BlockSpec((256, 512), lambda i: (0, jnp.maximum(i - 4, 0))),
            weights,
            weights,
        ],
        out_specs=(pl.BlockSpec((1024, 512), lambda i: (0, i)), whole),
        scratch_shapes=[pltpu.VMEM((2, 1024, 256), bf16), pltpu.VMEM((256, 1024), f32)],
        compiler_params=WHOLE,
        cost_estimate=takes(8),
        name="wide_grads",
    )(normed_two, grad_hidden, grad_mlp, activated, far(own_r), far(other_r))


def middle_back_kernel(
    middle_ref, mine_ref, swapped_ref, vectors_ref, gm_ref, own_ref, other_ref, out_ref, ga_ref, gheads_ref, cols_ref
):
    gm = gm_ref[...].astype(f32)
    norm, inverse = norm_parts(middle_ref[...])
    grad = mine_ref[...].astype(f32) + swapped_ref[...].astype(f32)
    out = gm + norm_back(grad, vectors_ref[3:4, :], norm, inverse)
    out_ref[...] = out
    low_out = low(out)
    ga_ref[...] = low_out
    field = dot(low_out[:, :512], own_ref[...]) + dot(low_out[:, 512:], other_ref[...])
    field = low(field).T
    for h in range(8):
        gheads_ref[h] = field[64 * h : 64 * (h + 1)]
    rows = [low_out.astype(f32), grad * norm, grad, gm]
    rows = [jnp.sum(r, axis=0, keepdims=True) for r in rows]
    cols_ref[...] = jnp.concatenate(rows + [jnp.zeros((4, 1024), f32)], axis=0)


def middle_back(middle, mine, swapped, vectors, grad_mlp, own, other):
    def whole(*dims):
        return pl.BlockSpec(dims, lambda i: (0,) * len(dims))

    wide = whole(256, 1024)
    return pl.pallas_call(
        middle_back_kernel,
        grid=(1,),
        out_shape=(
            shape(256, 1024, kind=f32),
            shape(256, 1024),
            shape(8, 64, 256),
            shape(8, 1024, kind=f32),
        ),
        in_specs=[wide, wide, wide, whole(8, 1024), wide, whole(512, 512), whole(512, 512)],
        out_specs=(wide, wide, whole(8, 64, 256), whole(8, 1024)),
        compiler_params=ROOMY,
        cost_estimate=takes(3),
        name="middle_back",
    )(middle, mine, swapped, vectors, grad_mlp, own, other)


def put_block(ref, at, block):
    for g in range(32):
        ref[16 * g : 16 * (g + 1), at : at + 128] = block


def merge_kernel(query_ref, own_ref, other_ref, out_ref):
    out_ref[:, :64, :] = query_ref[...]
    out_ref[:, 64:, :] = low(own_ref[...] + other_ref[...].astype(f32))


def final_kernel(
    lengths_ref, inputs_ref, middle_ref, mine_ref, swapped_ref, vectors_ref, out_ref, roots_ref, order_ref
):
    feature_order(order_ref)
    valid = valid_rows(lengths_ref)
    inputs = inputs_ref[...].astype(f32)
    middle = middle_ref[...]
    mlp_out = mine_ref[...].astype(f32) + swapped_ref[...].astype(f32) + vectors_ref[5:6, :]
    final = middle + mlp_out
    out_ref[...] = low(contract(low(final), order_ref[...], 1, 1))
    lane = lax.broadcasted_iota(jnp.int32, (1, 128), 1)
    total = jnp.zeros((1, 128), f32)
    for k, field in enumerate((inputs, middle - inputs, mlp_out, final)):
        total = jnp.where(lane == k, jnp.sum(valid * field * field), total)
    roots_ref[...] = total


def side_kernel(ga_ref, heads_ref, rows_ref, mine_ref, theirs_ref):
    cols = jnp.concatenate([rows_ref[...], jnp.zeros((120, 1024), f32)], axis=0)
    for half, ref in ((0, mine_ref), (1, theirs_ref)):
        rows = slice(512 * half, 512 * (half + 1))
        ref[:, :512] = low(contract(ga_ref[:, rows].T, heads_ref[...], 1, 1))
        ref[:, 512:] = low(cols[:, rows].T)


def side_add_kernel(a_ref, b_ref, out_ref):
    out_ref[...] = low(a_ref[...].astype(f32) + b_ref[...].astype(f32))


def back_kernel(
    gback_ref,
    own_ref,
    other_ref,
    normed_ref,
    inputs_ref,
    roots_ref,
    gh_ref,
    part_ref,
    mine_ref,
    theirs_ref,
    rows_ref,
    grads_ref,
):
    for c in range(3):
        for h in range(8):
            at = 512 * c + 64 * h
            grads_ref[at : at + 64, :] = gback_ref[h, 64 * c : 64 * (c + 1), :]
    left = normed_ref[...].T
    more = contract(jnp.ones((8, 256), bf16), gh_ref[...], 1, 0)[0:1]
    more = low(jnp.concatenate([more[:, 128 * r : 128 * (r + 1)] for r in range(16)], axis=0))
    sums = contract(jnp.ones((8, 256), bf16), grads_ref[...], 1, 1)[0:1]
    sums = [sums[:, 128 * r : 128 * (r + 1)] for r in range(12)]
    sums = low(jnp.concatenate(sums + [roots_ref[...], jnp.zeros((3, 128), f32)], axis=0))
    for half, ref in ((0, mine_ref), (1, theirs_ref)):
        rows = slice(512 * half, 512 * (half + 1))
        for c in range(3):
            cols = slice(512 * c, 512 * (c + 1))
            ref[:, cols] = low(contract(left[rows], grads_ref[cols, :], 1, 1))
        put_block(ref, 1536, sums)
        put_block(ref, 1664, more)
    sides = [grads_ref[512 * c : 512 * (c + 1), :].T for c in range(3)]
    norm, _ = norm_parts(inputs_ref[...].astype(f32))
    for half, ref in ((0, own_ref), (1, other_ref)):
        rows = slice(512 * half, 512 * (half + 1))
        part = sum(contract(sides[c], ref[:, 512 * (c + 1) : 512 * (c + 2)], 1, 1) for c in range(3))
        part = low(part)
        part_ref[:, rows] = part
        part = part.astype(f32)
        gain = jnp.sum(part * norm[:, rows], axis=0, keepdims=True)
        shift = jnp.sum(part, axis=0, keepdims=True)
        rows_ref[half] = jnp.concatenate([gain, shift, jnp.zeros((6, 512), f32)], axis=0)


def core_add_kernel(a_ref, b_ref, side_ref, rows_ref, c_ref, t_ref, d_ref, out_ref):
    out_ref[:, :1792] = low(a_ref[...].astype(f32) + b_ref[...].astype(f32))
    out_ref[:, 1792:2304] = side_ref[:, :512]
    ln1 = (rows_ref[...] + t_ref[...]) + (c_ref[...] + d_ref[...])
    ln1 = jnp.concatenate([jnp.zeros((4, 128), f32), ln1[:2], jnp.zeros((122, 128), f32)], axis=0)
    out_ref[:, 2304:] = low(side_ref[:, 512:].astype(f32) + ln1.T)


def core_add(mine, theirs, side, rows, by_core, by_tp, by_both):
    def tall(cols):
        return pl.BlockSpec((128, cols), lambda i: (i, 0))

    flat = pl.BlockSpec((8, 128), lambda i: (0, i))
    return pl.pallas_call(
        core_add_kernel,
        grid=(4,),
        out_shape=shape(512, 2432),
        in_specs=[tall(1792), tall(1792), tall(640), flat, flat, flat, flat],
        out_specs=tall(2432),
        compiler_params=ROOMY,
        cost_estimate=takes(2),
        name="qkv_core_sum",
    )(mine, theirs, side, rows, by_core, by_tp, by_both)


def end_kernel(inputs_ref, gmid_ref, mine_ref, swapped_ref, vectors_ref, out_ref, order_ref):
    feature_order(order_ref)
    norm, inverse = norm_parts(inputs_ref[...].astype(f32))
    grad = mine_ref[...].astype(f32) + swapped_ref[...].astype(f32)
    grad = gmid_ref[...] + norm_back(grad, vectors_ref[0:1, :], norm, inverse)
    out_ref[...] = low(contract(low(grad), order_ref[...], 1, 1))


def total_qkv_kernel(lengths_ref, got_ref, qkv_ref, proj_ref, bias_ref, fc_ref, cols_ref, roots_ref):
    total = got_ref[0].astype(f32)
    for k in range(1, 32):
        total = total + got_ref[k].astype(f32)
    for c in range(3):
        qkv_ref[:, c, :] = total[:, 512 * c : 512 * (c + 1)]
    for k in range(2):
        for r in range(4):
            row = 8 * k + r
            bias_ref[k : k + 1, 128 * r : 128 * (r + 1)] = total[row : row + 1, 1536:1664]
    count = lengths_ref[0] + lengths_ref[1] + lengths_ref[2] + lengths_ref[3]
    mean = total[12:13, 1536:1664] / (count.astype(f32) * 1024.0)
    roots_ref[...] = jnp.sqrt(mean + ROOT_EPS)
    fc_ref[...] = total[:, 1664:1792]
    proj_ref[...] = total[:, 1792:2304]
    cols_ref[...] = total[:, 2304:].T[:8]


def total_wide_kernel(mine_ref, theirs_ref, fc_ref, out_ref):
    total = mine_ref[...].astype(f32) + theirs_ref[...].astype(f32)
    fc_ref[...] = total[:, :2048]
    out_ref[...] = total[:, 2048:]


def body(
    tokens,
    ln1_gain,
    ln1_bias,
    qkv_weight,
    qv_bias,
    proj_weight,
    proj_bias,
    ln2_gain,
    ln2_bias,
    fc_weight,
    fc_bias,
    out_weight,
    out_bias,
    piece_starts,
    seq_lengths,
    cotangent,
):
    vectors = (ln1_gain, ln1_bias, proj_bias, ln2_gain, ln2_bias, out_bias)
    pay_q = call(
        prepare_kernel,
        "weights_payload",
        shape(32, 16, 2176),
        proj_weight.T,
        qkv_weight,
        *[v.reshape(1, 16) for v in vectors],
    )
    pay_r = call(
        prepare_rest_kernel,
        "rest_payload",
        shape(16, 4096),
        fc_weight,
        out_weight.T,
    )
    own_r = lax.all_gather(pay_r, SPREAD, axis=0, tiled=True)
    own_q = exchange(pay_q, SPREAD).reshape(512, 2176)
    inputs, grad_mlp = call(
        inputs_kernel,
        "inputs",
        (shape(256, 1024), shape(256, 1024)),
        seq_lengths,
        tokens[0],
        cotangent[0],
        scalars=1,
        cost=2,
        scratch=[pltpu.VMEM((1024, 1024), bf16)],
    )
    own_q = after(own_q, inputs)
    other_q = swap(own_q, "c")
    heads, normed, vectors = call(
        qkv_kernel,
        "qkv",
        (shape(8, 192, 256), shape(256, 1024), shape(8, 1024, kind=f32)),
        inputs,
        own_q,
        other_q,
        qv_bias,
        cost=3,
    )
    own = exchange(heads, LINE)
    other = swap(own[:, 64:], "c")
    attended, attended_low, log_sum = attn_forward(seq_lengths, piece_starts, own, other)
    heads_out = exchange(attended_low, LINE).reshape(512, 256)

    attn_part = project_out(heads_out, far(own_q), far(other_q))
    own_r = after(own_r, attn_part)
    other_r = swap(own_r, "c")
    grad_act = grad_activated(grad_mlp, own_r)
    middle, normed_two, activated, grad_hidden, two_part = feed_forward(
        inputs,
        attn_part,
        swap(attn_part, "tp"),
        vectors,
        grad_act,
        grad_mlp,
        fc_bias.reshape(1, 2048),
        own_r,
        other_r,
    )
    two_swapped = swap(two_part, "tp")
    wide, mlp_part = wide_grads(normed_two, grad_hidden, grad_mlp, activated, own_r, other_r)
    wide = lax.psum_scatter(after(wide, two_swapped), "c", scatter_dimension=0, tiled=True)
    two_swapped = after(two_swapped, mlp_part)
    grad_middle, grad_attn, grad_heads, rows = middle_back(
        middle, two_part, two_swapped, vectors, grad_mlp, far(own_q), far(other_q)
    )
    grad_mine = exchange(grad_heads, LINE)

    mine_p, theirs_p = call(
        side_kernel,
        "proj_grads",
        (shape(512, 640), shape(512, 640)),
        grad_attn,
        far(heads_out),
        rows,
        cost=2,
    )
    side = call(side_add_kernel, "proj_core_sum", shape(512, 640), mine_p, swap(theirs_p, "c"))
    grad_mine = after(grad_mine, side)
    mlp_swapped = swap(after(mlp_part, grad_mine), "tp")

    wide = lax.psum_scatter(after(wide, grad_mine), "x", scatter_dimension=0, tiled=True)
    grad_query, grad_own, grad_other = attn_backward(
        seq_lengths, piece_starts, own, other, grad_mine, attended, log_sum
    )
    grad_other, mlp_swapped = lax.optimization_barrier((grad_other, mlp_swapped))
    grad_back = call(
        merge_kernel, "merge", shape(8, 192, 256), grad_query, grad_own, swap(grad_other, "c")
    )
    grad_back = exchange(grad_back, LINE)
    layer_out, roots = call(
        final_kernel,
        "final",
        (shape(256, 1024), shape(1, 128, kind=f32)),
        seq_lengths,
        far(inputs),
        far(middle),
        after(mlp_part, grad_other),
        mlp_swapped,
        vectors,
        scalars=1,
        cost=3,
        scratch=[pltpu.VMEM((1024, 1024), bf16)],
    )
    wide = lax.psum_scatter(after(wide, roots), "y", scatter_dimension=0, tiled=True)
    one_part, mine_q, theirs_q, rows = call(
        back_kernel,
        "back",
        (
            shape(256, 1024),
            shape(512, 1792),
            shape(512, 1792),
            shape(2, 8, 512, kind=f32),
        ),
        grad_back,
        far(own_q),
        far(other_q),
        far(normed),
        far(inputs),
        roots,
        far(grad_hidden),
        cost=4,
        scratch=[pltpu.VMEM((1536, 256), bf16)],
    )
    both = core_add(
        mine_q,
        swap(theirs_q, "c"),
        side,
        rows[0],
        swap(rows[1], "c"),
        swap(rows[0], "tp"),
        lax.ppermute(rows[1], ("c", "tp"), [(i, 3 - i) for i in range(4)]),
    )
    got_q = exchange(both.reshape(32, 16, 2432), SPREAD)
    grad_tokens = call(
        end_kernel,
        "end",
        shape(256, 1024),
        far(inputs),
        far(grad_middle),
        far(one_part),
        swap(one_part, "tp"),
        vectors,
        cost=3,
        scratch=[pltpu.VMEM((1024, 1024), bf16)],
    )
    zh = lax.axis_index("zh")
    keep = lax.dynamic_slice_in_dim(wide, zh * 16, 16, 0)
    send = lax.dynamic_slice_in_dim(wide, 16 - zh * 16, 16, 0)
    grad_fc, grad_out = call(
        total_wide_kernel,
        "total_wide",
        (shape(16, 2048, kind=f32), shape(16, 2048, kind=f32)),
        keep,
        swap(send, "zh"),
    )
    got_q = after(got_q, grad_fc, grad_tokens)
    grad_qkv, grad_proj, bias_sums, fc_sums, cols, roots = call(
        total_qkv_kernel,
        "total_qkv",
        (
            shape(16, 3, 512, kind=f32),
            shape(16, 512, kind=f32),
            shape(2, 512, kind=f32),
            shape(16, 128, kind=f32),
            shape(8, 16, kind=f32),
            shape(1, 128, kind=f32),
        ),
        seq_lengths,
        got_q,
        scalars=1,
    )
    return (
        layer_out[None],
        grad_tokens[None],
        cols[4],
        cols[5],
        grad_qkv,
        bias_sums,
        grad_proj.T,
        cols[0],
        cols[1],
        cols[2],
        grad_fc,
        fc_sums.reshape(2048),
        grad_out.T,
        cols[3],
        roots[0, :4],
    )


def solution(mesh):
    fine = Mesh(mesh.devices.reshape(4, 2, 4, 2, 2), ("x", "zh", "y", "c", "tp"))
    ctx = ("zh", "y", "c")
    every = ("x", "zh", "y", "c")
    in_specs = (
        P("x", ctx, None),
        P(every),
        P(every),
        P(every, None, "tp"),
        P(None, "tp"),
        P("tp", every),
        P(every),
        P(every),
        P(every),
        P(every, "tp"),
        P("tp"),
        P("tp", every),
        P(every),
        P("x", None),
        P(),
        P("x", ctx, None),
    )
    out_specs = (
        P("x", ctx, None),
        P("x", ctx, None),
        P(every),
        P(every),
        P(every, None, "tp"),
        P(None, "tp"),
        P("tp", every),
        P(every),
        P(every),
        P(every),
        P(every, "tp"),
        P("tp"),
        P("tp", every),
        P(every),
        P(),
    )
    return jax.shard_map(body, mesh=fine, in_specs=in_specs, out_specs=out_specs, check_vma=False)
```

time: 486 us -> 312 us (0.64)
  blocking collectives: 92.4 us -> 33.4 us
  Pallas kernels: 43.8 us -> 96.6 us
  matrix products: 51.5 us -> 0 us
  waiting for transfers between devices: 157 us -> 106 us
  local copies, waits for them, and re-layouts: 63.5 us -> 26.9 us
  other arithmetic: 35.1 us -> 0 us
  between operations: 1.91 us -> 14.3 us
    all_to_all x3 -> x2, blocking collectives: 92.4 us -> 33.4 us  [exchange(): return lax.all_to_all(field, axes, split_axis=0, concat_axis=0, tiled=True)]
    all_to_all x5 -> x4, waiting for transfers between devices: 105 us -> 47.6 us  [exchange(): return lax.all_to_all(field, axes, split_axis=0, concat_axis=0, tiled=True)]
    pallas_call x0 -> x18, Pallas kernels: none -> 53.5 us  [the longest x12 24.3 us: call(): pl.pallas_call(kernel, grid=(1,), out_shape=outs, in_specs=[SM] * scalars...]
    dot_general x16 -> x0, matrix products: 51.5 us -> none  [the longest x12 40.6 us: contract(): lax.dot_general(a, b, (((dim_a,), (dim_b,)), ((), ())), preferred_element...]
    concatenate x3 -> x0, local copies, waits for them, and re-layouts: 30.4 us -> none  [the longest x1 22 us: body(): jnp.concatenate([grad_proj, grad_fc, grad_out, shared, columns, jnp.zeros...]
    unnamed x60 -> x92, local copies, waits for them, and re-layouts: 1.3 us -> 24.8 us
    reduce_sum x10 -> x0, other arithmetic: 13.8 us -> none  [the longest x2 4.92 us: scatter(): return jnp.sum(got.astype(f32), axis=0)]
    convert_element_type x5 -> x0, other arithmetic: 12.8 us -> none  [the longest x3 12.1 us: low(): return field.astype(bf16)]
  transfers between devices with their start and end apart: 16 -> 22, of which waited for: 13 -> 14; matrix products, arithmetic and copies ran while one was open for 16% -> 0% of each run, Pallas kernels for 4% -> 28%
where the time goes in v2:
time: 312 us; the launch traced here: 310 us
  waiting for transfers between devices  106 us (34%)
  Pallas kernels  96.6 us (31%)
  blocking collectives  33.4 us (11%)
  starting transfers between devices  33 us (11%)
  local copies, waits for them, and re-layouts  26.9 us (9%)
  between operations  14.3 us (5%)
    ppermute x13, waiting for transfers between devices, swap(): return lax.ppermute(field, axis, [(0, 1), (1, 0)])  54.7 us
    all_to_all x4, waiting for transfers between devices, exchange(): return lax.all_to_all(field, axes, split_axis=0, concat_axis=0, tiled=True)  47.6 us
    all_to_all x2, blocking collectives, exchange(): return lax.all_to_all(field, axes, split_axis=0, concat_axis=0, tiled=True)  33.4 us
    pallas_call x1, Pallas kernels, attn_backward(): pl.pallas_call(backward_kernel, out_shape=(jax.ShapeDtypeStruct((H, E, B)...  25 us
    unnamed x92, local copies, waits for them, and re-layouts  24.8 us
    pallas_call x12, Pallas kernels, call(): pl.pallas_call(kernel, grid=(1,), out_shape=outs, in_specs=[SM] * scalars...  24.3 us
    all_to_all x4, starting transfers between devices, exchange(): return lax.all_to_all(field, axes, split_axis=0, concat_axis=0, tiled=True)  23.5 us
    pallas_call x1, Pallas kernels, attn_forward(): pl.pallas_call(forward_kernel, out_shape=(jax.ShapeDtypeStruct((H, E, B),...  18 us
  transfers between devices with their start and end apart: 22, of which 14 were waited for; matrix products, arithmetic and copies ran while one was open for 0% of the time, Pallas kernels for 28%

profile of v2, /device:TPU:0, one launch (start us, length us, event | category | flops | bytes accessed | tf_op | source)
XLA Modules:
  0.0 310.1 jit_solution(10785920066828877335)
XLA Ops:
  9.8 3.0 weights_payload.1
  12.8 1.3 copy-done.2
  14.2 10.8 %all-to-all-start = ((bf16[32,16,2176]{2,1,0:T(8,128)(2,1)}), bf16[32,16,2176]{2,1,0:T(8,128)(2,1)S(1)}, u32[]{:S(2)}, u32[]{:S(2)}) async-start(bf16[32,16,2176]{2,1,0:T(8,128)(2,1)} %copy-done.2), calls=%async_computation | async-start | bytes 4456448 | tf_op jit(solution)/shard_map/all_to_all | solution.py:176
  25.1 1.9 inputs.1
  28.7 29.0 %all-to-all-done = bf16[32,16,2176]{2,1,0:T(8,128)(2,1)S(1)} async-done(((bf16[32,16,2176]{2,1,0:T(8,128)(2,1)}), bf16[32,16,2176]{2,1,0:T(8,128)(2,1)S(1)}, u32[]{:S(2)}, u32[]{:S(2)}) %all-to-all-start) | async-done | bytes 2228256 | tf_op jit(solution)/shard_map/all_to_all | solution.py:176
  57.7 4.3 %collective-permute-done.other_ref = bf16[512,2176]{1,0:T(8,128)(2,1)S(1)} collective-permute-done((bf16[512,2176]{1,0:T(8,128)(2,1)S(1)}, bf16[512,2176]{1,0:T(8,128)(2,1)S(1)}, u32[]{:S(2)}, u32[]{:S(2)}) %collective-permute-start) | collective-permute-done | bytes 2228256 | tf_op jit(solution)/shard_map/ppermute | solution.py:172
  62.0 1.1 copy-done.35
  63.2 1.4 qkv.1
  64.6 19.9 %all_to_all.30.own_ref = bf16[8,192,256]{2,1,0:T(8,128)(2,1)S(1)} all-to-all(bf16[8,192,256]{2,1,0:T(8,128)(2,1)S(1)} %get-tuple-element.67), channel_id=1, replica_groups=mesh['x'=4,'zh'=2,'y'=4,'c'=2,'tp'=2] {'zh','y'}, dimensions={0} | all-to-all | bytes 1572864 | tf_op jit(solution)/shard_map/all_to_all | solution.py:176
  84.6 1.9 collective-permute-done.1.other_ref
  86.5 18.0 %attention_forward.1 = (f32[8,64,256]{2,1,0:T(8,128)S(1)}, bf16[8,64,256]{2,1,0:T(8,128)(2,1)S(1)}, f32[8,1,256]{2,1,0:T(1,128)S(1)}) custom-call(s32[4]{0:T(128)S(1)} %copy-done.20, s32[1,2]{1,0:T(1,128)S(1)} %copy-done.19, bf16[8,192,256]{2,1,0:T(8,128)(2,1)S(1)} %all_to_all.30.own_ref, bf16[8,128,256]{2,1,0:T(8,128)(2,1)S(1)} %collective-permute-done.1.other_ref), custom_call_target="tpu_custom_call" | custom-call | flops 4600000000 | bytes 1048576 | tf_op jit(solution)/shard_map/attention_forward/pallas_call | solution.py:134
  104.6 13.6 %all_to_all.31 = bf16[8,64,256]{2,1,0:T(8,128)(2,1)S(1)} all-to-all(bf16[8,64,256]{2,1,0:T(8,128)(2,1)S(1)} %get-tuple-element.68), channel_id=1, replica_groups=mesh['x'=4,'zh'=2,'y'=4,'c'=2,'tp'=2] {'zh','y'}, dimensions={0} | all-to-all | bytes 524288 | tf_op jit(solution)/shard_map/all_to_all | solution.py:176
  118.1 1.8 proj.1.mine_ref
  120.1 1.2 collective-permute-start.2
  121.3 3.3 %grad_act.1.gact_ref = f32[256,2048]{1,0:T(8,128)S(1)} custom-call(bf16[256,1024]{1,0:T(8,128)(2,1)S(1)} %copy-done.26, bf16[512,4096]{1,0:T(8,128)(2,1)} %all-gather.2.cloned.1.call-done.own_ref), custom_call_target="tpu_custom_call" | custom-call | flops 2300000000 | bytes 1048576 | tf_op jit(solution)/shard_map/grad_act/pallas_call | solution.py:323
  124.5 9.9 %collective-permute-done.2.swapped_ref = bf16[256,1024]{1,0:T(8,128)(2,1)S(1)} collective-permute-done((bf16[256,1024]{1,0:T(8,128)(2,1)S(1)}, bf16[256,1024]{1,0:T(8,128)(2,1)S(1)}, u32[]{:S(2)}, u32[]{:S(2)}) %collective-permute-start.2) | collective-permute-done | bytes 524320 | tf_op jit(solution)/shard_map/ppermute | solution.py:172
  134.4 1.9 copy-done.44
  136.4 7.0 %feed_forward.1 = (f32[256,1024]{1,0:T(8,128)S(1)}, bf16[256,1024]{1,0:T(8,128)(2,1)S(1)}, bf16[256,2048]{1,0:T(8,128)(2,1)S(1)}, bf16[256,2048]{1,0:T(8,128)(2,1)S(1)}, bf16[256,1024]{1,0:T(8,128)(2,1)S(1)}) custom-call(bf16[256,1024]{1,0:T(8,128)(2,1)S(1)} %copy-done.36, bf16[256,1024]{1,0:T(8,128)(2,1)S(1)} %proj.1.mine_ref, ...), custom_call_target="tpu_custom_call" | custom-call | flops 9200000000 | bytes 1048576 | tf_op jit(solution)/shard_map/feed_forward/pallas_call | solution.py:395
  145.3 1.1 copy-done.38
  147.2 1.1 collective-permute-start.4
  148.2 11.2 %wide_grads.1 = (bf16[1024,4096]{1,0:T(8,128)(2,1)}, bf16[256,1024]{1,0:T(8,128)(2,1)}) custom-call(bf16[256,1024]{1,0:T(8,128)(2,1)} %copy-done.41, bf16[256,2048]{1,0:T(8,128)(2,1)} %copy-done.33, bf16[256,1024]{1,0:T(8,128)(2,1)} %copy-done.25, bf16[256,2048]{1,0:T(8,128)(2,1)} %copy-done.38, bf16[512,4096]{1,0:T(8,128)(2,1)} %all-gather.2.cloned.1.call-done.own_ref, ...), custom_call_target="tpu_custom_call" | custom-call | flops 9200000000 | bytes 1048576 | tf_op jit(solution)/shard_map/wide_grads/pallas_call | solution.py:471
  159.4 1.2 collective-permute-done.4.swapped_ref
  161.7 1.2 copy-done.32
  162.9 3.2 %middle_back.1 = (f32[256,1024]{1,0:T(8,128)S(1)}, bf16[256,1024]{1,0:T(8,128)(2,1)S(1)}, bf16[8,64,256]{2,1,0:T(8,128)(2,1)}, f32[8,1024]{1,0:T(8,128)S(1)}) custom-call(f32[256,1024]{1,0:T(8,128)S(1)} %copy-done.32, bf16[256,1024]{1,0:T(8,128)(2,1)S(1)} %get-tuple-element.77.mine_ref, bf16[256,1024]{1,0:T(8,128)(2,1)S(1)} %collective-permute-done.4.swapped_ref, ...), custom_call_target="tpu_custom_call" | custom-call | flops 3449999872 | bytes 1048576 | tf_op jit(solution)/shard_map/middle_back/pallas_call | solution.py:515
  167.1 1.4 proj_grads.1
  169.4 3.8 %all-to-all-start.3 = ((bf16[8,64,256]{2,1,0:T(8,128)(2,1)}), bf16[8,64,256]{2,1,0:T(8,128)(2,1)S(1)}, u32[]{:S(2)}, u32[]{:S(2)}) async-start(bf16[8,64,256]{2,1,0:T(8,128)(2,1)} %get-tuple-element.79), calls=%async_computation.3 | async-start | bytes 524288 | tf_op jit(solution)/shard_map/all_to_all | solution.py:176
  173.4 1.2 copy-done.29
  175.6 7.0 %all-to-all-done.3.gout_ref = bf16[8,64,256]{2,1,0:T(8,128)(2,1)S(1)} async-done(((bf16[8,64,256]{2,1,0:T(8,128)(2,1)}), bf16[8,64,256]{2,1,0:T(8,128)(2,1)S(1)}, u32[]{:S(2)}, u32[]{:S(2)}) %all-to-all-start.3) | async-done | bytes 262176 | tf_op jit(solution)/shard_map/all_to_all | solution.py:176
  183.7 1.0 copy-done.40
  184.8 25.0 %attention_backward.1 = (bf16[8,64,256]{2,1,0:T(8,128)(2,1)S(1)}, f32[8,128,256]{2,1,0:T(8,128)S(1)}, bf16[8,128,256]{2,1,0:T(8,128)(2,1)S(1)}) custom-call(s32[4]{0:T(128)S(1)} %copy-done.20, s32[1,2]{1,0:T(1,128)S(1)} %copy-done.19, bf16[8,192,256]{2,1,0:T(8,128)(2,1)S(1)} %all_to_all.30.own_ref, ...), custom_call_target="tpu_custom_call" | custom-call | flops 29899999232 | bytes 1048576 | tf_op jit(solution)/shard_map/attention_backward/pallas_call | solution.py:143
  210.2 1.6 collective-permute-done.7.other_ref
  212.8 3.6 %all-to-all-start.4 = ((bf16[8,192,256]{2,1,0:T(8,128)(2,1)}), bf16[8,192,256]{2,1,0:T(8,128)(2,1)S(1)}, u32[]{:S(2)}, u32[]{:S(2)}) async-start(bf16[8,192,256]{2,1,0:T(8,128)(2,1)} %merge.1), calls=%async_computation.4 | async-start | bytes 1572864 | tf_op jit(solution)/shard_map/all_to_all | solution.py:176
  216.4 3.4 %final.1 = (bf16[256,1024]{1,0:T(8,128)(2,1)}, f32[1,128]{1,0:T(1,128)S(1)}) custom-call(s32[4]{0:T(128)S(1)} %copy-done.20, bf16[256,1024]{1,0:T(8,128)(2,1)} %copy-done.34, f32[256,1024]{1,0:T(8,128)} %copy-done.31, bf16[256,1024]{1,0:T(8,128)(2,1)S(1)} %copy-done.8, bf16[256,1024]{1,0:T(8,128)(2,1)S(1)} %collective-permute-done.6.swapped_ref, ...), custom_call_target="tpu_custom_call" | custom-call | flops 3449999872 | bytes 1048576 | tf_op jit(solution)/shard_map/final/pallas_call | solution.py:201
  219.8 11.6 %all-to-all-done.4.gback_ref = bf16[8,192,256]{2,1,0:T(8,128)(2,1)S(1)} async-done(((bf16[8,192,256]{2,1,0:T(8,128)(2,1)}), bf16[8,192,256]{2,1,0:T(8,128)(2,1)S(1)}, u32[]{:S(2)}, u32[]{:S(2)}) %all-to-all-start.4) | async-done | bytes 786464 | tf_op jit(solution)/shard_map/all_to_all | solution.py:176
  231.4 5.1 %back.1 = (bf16[256,1024]{1,0:T(8,128)(2,1)S(1)}, bf16[512,1792]{1,0:T(8,128)(2,1)S(1)}, bf16[512,1792]{1,0:T(8,128)(2,1)S(1)}, f32[2,8,512]{2,1,0:T(8,128)S(1)}) custom-call(bf16[8,192,256]{2,1,0:T(8,128)(2,1)S(1)} %all-to-all-done.4.gback_ref, bf16[512,2176]{1,0:T(8,128)(2,1)} %bitcast.41, bf16[512,2176]{1,0:T(8,128)(2,1)} %copy-done.4, ...), custom_call_target="tpu_custom_call" | custom-call | flops 4600000000 | bytes 1048576 | tf_op jit(solution)/shard_map/back/pallas_call | solution.py:201
  236.6 1.2 copy-done.21
  239.8 1.4 collective-permute-done.10.c_ref
  242.7 1.6 copy-done.22
  244.3 1.1 copy-done.24
  245.4 2.9 qkv_core_sum.1
  248.3 1.4 copy-done
  249.7 5.3 %all-to-all-start.5 = ((bf16[32,16,2432]{2,1,0:T(8,128)(2,1)}), bf16[32,16,2432]{2,1,0:T(8,128)(2,1)S(1)}, u32[]{:S(2)}, u32[]{:S(2)}) async-start(bf16[32,16,2432]{2,1,0:T(8,128)(2,1)} %bitcast.36), calls=%async_computation.5 | async-start | bytes 4980736 | tf_op jit(solution)/shard_map/all_to_all | solution.py:176
  255.1 3.0 reduce-scatter.8.cloned.1.call-done
  259.1 3.2 %collective-permute-start.13 = (bf16[16,4096]{1,0:T(8,128)(2,1)S(1)}, bf16[16,4096]{1,0:T(8,128)(2,1)S(1)}, u32[]{:S(2)}, u32[]{:S(2)}) collective-permute-start(bf16[16,4096]{1,0:T(8,128)(2,1)S(1)} %get-tuple-element.130), channel_id=1, source_target_pairs={{0,16},{16,0},{1,17},{17,1},{2,18},{18,2},{3,19},{19,3},{4,20},{20... | collective-permute-start | bytes 393224 | tf_op jit(solution)/shard_map/ppermute | solution.py:172
  262.3 32.1 %collective-permute-done.8.swapped_ref = bf16[256,1024]{1,0:T(8,128)(2,1)} collective-permute-done((bf16[256,1024]{1,0:T(8,128)(2,1)S(1)}, bf16[256,1024]{1,0:T(8,128)(2,1)}, u32[]{:S(2)}, u32[]{:S(2)}) %collective-permute-start.8) | collective-permute-done | bytes 524320 | tf_op jit(solution)/shard_map/ppermute | solution.py:172
  294.5 3.9 %end.1 = bf16[256,1024]{1,0:T(8,128)(2,1)} custom-call(bf16[256,1024]{1,0:T(8,128)(2,1)} %copy-done.34, f32[256,1024]{1,0:T(8,128)} %copy-done.30, bf16[256,1024]{1,0:T(8,128)(2,1)} %copy-done.7, bf16[256,1024]{1,0:T(8,128)(2,1)} %collective-permute-done.8.swapped_ref, f32[8,1024]{1,0:T(8,128)S(1)} %get-tuple-element.69.vectors_ref), custom_call_target="tpu_custom_call" | custom-call | flops 3449999872 | bytes 1048576 | tf_op jit(solution)/shard_map/end/pallas_call | solution.py:201
  298.4 1.2 collective-permute-done.13.theirs_ref
  300.3 1.6 total_qkv.1
  (120 shorter events, 20.8 us)
Async XLA Ops:
  7.2 112.8 %all-gather.2.cloned.1.call-start = ((), (), s32[]{:S(2)}) async-start(), calls=%async_computation.9 | async-start | bytes 4325376 | tf_op jit(solution)/shard_map/all_gather | solution.py:706
  12.8 1.3 copy-start.2
  14.2 10.9 %copy-start.5 = (bf16[1,256,1024]{2,1,0:T(8,128)(2,1)S(1)}, bf16[1,256,1024]{2,1,0:T(8,128)(2,1)}, u32[]{:S(2)}) copy-start(bf16[1,256,1024]{2,1,0:T(8,128)(2,1)} %param.16) | copy-start | bytes 1572868
  14.2 10.9 %copy-start.6 = (bf16[1,256,1024]{2,1,0:T(8,128)(2,1)S(1)}, bf16[1,256,1024]{2,1,0:T(8,128)(2,1)}, u32[]{:S(2)}) copy-start(bf16[1,256,1024]{2,1,0:T(8,128)(2,1)} %param.31) | copy-start | bytes 1572868
  14.2 10.9 %copy-start.20 = (s32[4]{0:T(128)S(1)}, s32[4]{0:T(128)}, u32[]{:S(2)}) copy-start(s32[4]{0:T(128)} %lengths_ref.9) | copy-start | bytes 52
  14.2 43.5 %all-to-all-start = ((bf16[32,16,2176]{2,1,0:T(8,128)(2,1)}), bf16[32,16,2176]{2,1,0:T(8,128)(2,1)S(1)}, u32[]{:S(2)}, u32[]{:S(2)}) async-start(bf16[32,16,2176]{2,1,0:T(8,128)(2,1)} %copy-done.2), calls=%async_computation | async-start | bytes 4456448 | tf_op jit(solution)/shard_map/all_to_all | solution.py:176
  25.0 157.6 %reduce-scatter.4.cloned.1.call-start = ((), (), s32[]{:S(2)}) async-start(), calls=%async_computation.10 | async-start | bytes 12582912 | tf_op jit(solution)/shard_map/reduce_scatter | solution.py:753
  25.1 36.9 %copy-start.12 = (bf16[2,512]{1,0:T(2,128)(2,1)S(1)}, bf16[2,512]{1,0:T(2,128)(2,1)}, u32[]{:S(2)}) copy-start(bf16[2,512]{1,0:T(2,128)(2,1)} %bias_ref.1) | copy-start | bytes 6148
  57.7 6.9 %copy-start.1 = (bf16[32,16,2176]{2,1,0:T(8,128)(2,1)}, bf16[32,16,2176]{2,1,0:T(8,128)(2,1)S(1)}, u32[]{:S(2)}) copy-start(bf16[32,16,2176]{2,1,0:T(8,128)(2,1)S(1)} %all-to-all-done) | copy-start | bytes 6684676
  57.7 4.3 %collective-permute-start = (bf16[512,2176]{1,0:T(8,128)(2,1)S(1)}, bf16[512,2176]{1,0:T(8,128)(2,1)S(1)}, u32[]{:S(2)}, u32[]{:S(2)}) collective-permute-start(bf16[512,2176]{1,0:T(8,128)(2,1)S(1)} %bitcast.37), channel_id=1, source_target_pairs={{0,2},{2,0},{1,3},{3,1},{4,6},{6,4},{5,7},{7,5},{8,10},{10,8},{9,1... | collective-permute-start | bytes 6684680 | tf_op jit(solution)/shard_map/ppermute | solution.py:172
  62.0 1.1 copy-start.35
  63.2 1.4 copy-start.4
  64.6 39.9 %copy-start.37 = (bf16[256,1024]{1,0:T(8,128)(2,1)}, bf16[256,1024]{1,0:T(8,128)(2,1)S(1)}, u32[]{:S(2)}) copy-start(bf16[256,1024]{1,0:T(8,128)(2,1)S(1)} %get-tuple-element.96.normed_ref) | copy-start | bytes 1572868
  64.6 21.9 %copy-start.19 = (s32[1,2]{1,0:T(1,128)S(1)}, s32[1,2]{1,0:T(1,128)}, u32[]{:S(2)}) copy-start(s32[1,2]{1,0:T(1,128)} %starts_ref.3) | copy-start | bytes 28
  84.5 2.0 collective-permute-start.1
  104.6 13.6 %copy-start.39 = (f32[8,64,256]{2,1,0:T(8,128)}, f32[8,64,256]{2,1,0:T(8,128)S(1)}, u32[]{:S(2)}) copy-start(f32[8,64,256]{2,1,0:T(8,128)S(1)} %get-tuple-element.85.out_ref) | copy-start | bytes 1572868
  118.1 1.8 copy-start.3
  118.1 3.1 copy-start.43
  118.1 3.1 %copy-start.26 = (bf16[256,1024]{1,0:T(8,128)(2,1)S(1)}, bf16[256,1024]{1,0:T(8,128)(2,1)}, u32[]{:S(2)}) copy-start(bf16[256,1024]{1,0:T(8,128)(2,1)} %copy-done.25) | copy-start | bytes 1572868
  120.0 14.4 %collective-permute-start.3 = (bf16[512,4096]{1,0:T(8,128)(2,1)}, bf16[512,4096]{1,0:T(8,128)(2,1)S(1)}, u32[]{:S(2)}, u32[]{:S(2)}) collective-permute-start(bf16[512,4096]{1,0:T(8,128)(2,1)} %all-gather.2.cloned.1.call-done.own_ref), channel_id=1, source_target_pairs={{0,2},{2,0},{1,3},{3,1},{4,6},{6,4},{5,7},{7,5},{8,10},{10,8},{9,1... | collective-permute-start | bytes 12582920 | tf_op jit(solution)/shard_map/ppermute | solution.py:172
  120.1 14.3 %collective-permute-start.2 = (bf16[256,1024]{1,0:T(8,128)(2,1)S(1)}, bf16[256,1024]{1,0:T(8,128)(2,1)S(1)}, u32[]{:S(2)}, u32[]{:S(2)}) collective-permute-start(bf16[256,1024]{1,0:T(8,128)(2,1)S(1)} %proj.1.mine_ref), channel_id=1, source_target_pairs={{0,1},{1,0},{2,3},{3,2},{4,5},{5,4},{6,7},{7,6},{8,9},{9,8},{10,11... | collective-permute-start | bytes 1572872 | tf_op jit(solution)/shard_map/ppermute | solution.py:172
  121.2 15.1 %copy-start.36 = (bf16[256,1024]{1,0:T(8,128)(2,1)S(1)}, bf16[256,1024]{1,0:T(8,128)(2,1)}, u32[]{:S(2)}) copy-start(bf16[256,1024]{1,0:T(8,128)(2,1)} %copy-done.34) | copy-start | bytes 1572868
  134.4 1.9 copy-start.44
  145.3 1.1 copy-start.38
  147.2 13.5 %collective-permute-start.4 = (bf16[256,1024]{1,0:T(8,128)(2,1)S(1)}, bf16[256,1024]{1,0:T(8,128)(2,1)S(1)}, u32[]{:S(2)}, u32[]{:S(2)}) collective-permute-start(bf16[256,1024]{1,0:T(8,128)(2,1)S(1)} %get-tuple-element.77.mine_ref), channel_id=1, source_target_pairs={{0,1},{1,0},{2,3},{3,2},{4,5},{5,4},{6,7},{7,6},{8,9},{9,8},{10,11... | collective-permute-start | bytes 1572872 | tf_op jit(solution)/shard_map/ppermute | solution.py:172
  160.6 1.0 copy-start.27
  161.7 1.2 copy-start.32
  169.4 4.1 %collective-permute-start.5 = (bf16[512,640]{1,0:T(8,128)(2,1)S(1)}, bf16[512,640]{1,0:T(8,128)(2,1)S(1)}, u32[]{:S(2)}, u32[]{:S(2)}) collective-permute-start(bf16[512,640]{1,0:T(8,128)(2,1)S(1)} %get-tuple-element.83), channel_id=1, source_target_pairs={{0,2},{2,0},{1,3},{3,1},{4,6},{6,4},{5,7},{7,5},{8,10},{10,8},{9,1... | collective-permute-start | bytes 1966088 | tf_op jit(solution)/shard_map/ppermute | solution.py:172
  169.4 13.3 %all-to-all-start.3 = ((bf16[8,64,256]{2,1,0:T(8,128)(2,1)}), bf16[8,64,256]{2,1,0:T(8,128)(2,1)S(1)}, u32[]{:S(2)}, u32[]{:S(2)}) async-start(bf16[8,64,256]{2,1,0:T(8,128)(2,1)} %get-tuple-element.79), calls=%async_computation.3 | async-start | bytes 524288 | tf_op jit(solution)/shard_map/all_to_all | solution.py:176
  173.2 64.6 %reduce-scatter.6.cloned.1.call-start = ((), (), s32[]{:S(2)}) async-start(), calls=%async_computation.11 | async-start | bytes 5242880 | tf_op jit(solution)/shard_map/reduce_scatter | solution.py:773
  173.4 1.2 copy-start.29
  175.6 7.1 %copy-start.8 = (bf16[256,1024]{1,0:T(8,128)(2,1)S(1)}, bf16[256,1024]{1,0:T(8,128)(2,1)}, u32[]{:S(2)}) copy-start(bf16[256,1024]{1,0:T(8,128)(2,1)} %get-tuple-element.90.mine_ref) | copy-start | bytes 1572868
  182.7 27.1 %collective-permute-start.6 = (bf16[256,1024]{1,0:T(8,128)(2,1)S(1)}, bf16[256,1024]{1,0:T(8,128)(2,1)S(1)}, u32[]{:S(2)}, u32[]{:S(2)}) collective-permute-start(bf16[256,1024]{1,0:T(8,128)(2,1)S(1)} %copy-done.8), channel_id=1, source_target_pairs={{0,1},{1,0},{2,3},{3,2},{4,5},{5,4},{6,7},{7,6},{8,9},{9,8},{10,11... | collective-permute-start | bytes 1572872 | tf_op jit(solution)/shard_map/ppermute | solution.py:172
  209.8 2.0 collective-permute-start.7
  212.8 18.6 %all-to-all-start.4 = ((bf16[8,192,256]{2,1,0:T(8,128)(2,1)}), bf16[8,192,256]{2,1,0:T(8,128)(2,1)S(1)}, u32[]{:S(2)}, u32[]{:S(2)}) async-start(bf16[8,192,256]{2,1,0:T(8,128)(2,1)} %merge.1), calls=%async_computation.4 | async-start | bytes 1572864 | tf_op jit(solution)/shard_map/all_to_all | solution.py:176
  216.3 41.8 %reduce-scatter.8.cloned.1.call-start = ((), (), s32[]{:S(2)}) async-start(), calls=%async_computation.12 | async-start | bytes 1310720 | tf_op jit(solution)/shard_map/reduce_scatter | solution.py:796
  236.5 1.2 copy-start.21
  237.8 17.2 %copy-start.7 = (bf16[256,1024]{1,0:T(8,128)(2,1)}, bf16[256,1024]{1,0:T(8,128)(2,1)S(1)}, u32[]{:S(2)}) copy-start(bf16[256,1024]{1,0:T(8,128)(2,1)S(1)} %get-tuple-element.98.mine_ref) | copy-start | bytes 1572868
  237.8 5.0 %collective-permute-start.9 = (bf16[512,1792]{1,0:T(8,128)(2,1)S(1)}, bf16[512,1792]{1,0:T(8,128)(2,1)}, u32[]{:S(2)}, u32[]{:S(2)}) collective-permute-start(bf16[512,1792]{1,0:T(8,128)(2,1)S(1)} %get-tuple-element.100), channel_id=1, source_target_pairs={{0,2},{2,0},{1,3},{3,1},{4,6},{6,4},{5,7},{7,5},{8,10},{10,8},{9,1... | collective-permute-start | bytes 5505032 | tf_op jit(solution)/shard_map/ppermute | solution.py:172
  237.8 3.4 %collective-permute-start.10 = (f32[8,512]{1,0:T(8,128)S(1)}, f32[8,512]{1,0:T(8,128)S(1)}, u32[]{:S(2)}, u32[]{:S(2)}) collective-permute-start(f32[8,512]{1,0:T(8,128)S(1)} %get-tuple-element.132), channel_id=1, source_target_pairs={{0,2},{2,0},{1,3},{3,1},{4,6},{6,4},{5,7},{7,5},{8,10},{10,8},{9,1... | collective-permute-start | bytes 49160 | tf_op jit(solution)/shard_map/ppermute | solution.py:172
  238.4 3.7 %collective-permute-start.11 = (f32[8,512]{1,0:T(8,128)S(1)}, f32[8,512]{1,0:T(8,128)S(1)}, u32[]{:S(2)}, u32[]{:S(2)}) collective-permute-start(f32[8,512]{1,0:T(8,128)S(1)} %get-tuple-element.133.rows_ref), channel_id=1, source_target_pairs={{0,1},{1,0},{2,3},{3,2},{4,5},{5,4},{6,7},{7,6},{8,9},{9,8},{10,11... | collective-permute-start | bytes 49160 | tf_op jit(solution)/shard_map/ppermute | solution.py:172
  239.4 3.3 %collective-permute-start.12 = (f32[8,512]{1,0:T(8,128)S(1)}, f32[8,512]{1,0:T(8,128)S(1)}, u32[]{:S(2)}, u32[]{:S(2)}) collective-permute-start(f32[8,512]{1,0:T(8,128)S(1)} %get-tuple-element.132), channel_id=1, source_target_pairs={{0,3},{1,2},{2,1},{3,0},{4,7},{5,6},{6,5},{7,4},{8,11},{9,10},{10,... | collective-permute-start | bytes 49160 | tf_op jit(solution)/shard_map/ppermute | solution.py:823
  242.7 1.6 copy-start.22
  244.3 1.1 copy-start.24
  248.2 1.4 copy-start
  249.7 50.6 %all-to-all-start.5 = ((bf16[32,16,2432]{2,1,0:T(8,128)(2,1)}), bf16[32,16,2432]{2,1,0:T(8,128)(2,1)S(1)}, u32[]{:S(2)}, u32[]{:S(2)}) async-start(bf16[32,16,2432]{2,1,0:T(8,128)(2,1)} %bitcast.36), calls=%async_computation.5 | async-start | bytes 4980736 | tf_op jit(solution)/shard_map/all_to_all | solution.py:176
  255.0 39.5 %collective-permute-start.8 = (bf16[256,1024]{1,0:T(8,128)(2,1)S(1)}, bf16[256,1024]{1,0:T(8,128)(2,1)}, u32[]{:S(2)}, u32[]{:S(2)}) collective-permute-start(bf16[256,1024]{1,0:T(8,128)(2,1)S(1)} %get-tuple-element.98.mine_ref), channel_id=1, source_target_pairs={{0,1},{1,0},{2,3},{3,2},{4,5},{5,4},{6,7},{7,6},{8,9},{9,8},{10,11... | collective-permute-start | bytes 1572872 | tf_op jit(solution)/shard_map/ppermute | solution.py:172
  259.1 40.5 %collective-permute-start.13 = (bf16[16,4096]{1,0:T(8,128)(2,1)S(1)}, bf16[16,4096]{1,0:T(8,128)(2,1)S(1)}, u32[]{:S(2)}, u32[]{:S(2)}) collective-permute-start(bf16[16,4096]{1,0:T(8,128)(2,1)S(1)} %get-tuple-element.130), channel_id=1, source_target_pairs={{0,16},{16,0},{1,17},{17,1},{2,18},{18,2},{3,19},{19,3},{4,20},{20... | collective-permute-start | bytes 393224 | tf_op jit(solution)/shard_map/ppermute | solution.py:172
  (19 other events, 16.6 us)
Sparse Core Ops, SparseCore 0:
  11.6 106.8 all-gather.1
  160.8 17.9 reduce-scatter.3
  182.8 46.0 reduce-scatter.5
  237.9 20.1 reduce-scatter.7
